TPU v7x, 256 devices: a whole 4x4x8 slice. The times are simulated.
256 devices in a mesh: segment: 2 (over core), space: 32 (over z, x), dp: 4 (over y).
Axes of the slice: x: 4, y: 4, z: 8, core: 2. Of those that a mesh axis runs over, the one named last changes fastest.
Arguments:
- latents: bfloat16 [8, 1, 128, 128, 320], P('dp', None, 'space'), may hold values from -14 to 14
- hint: bfloat16 [8, 1, 128, 128, 320], P('dp', None, 'space'), may hold values from -6 to 6
- cotangent: bfloat16 [8, 1, 128, 128, 320], P('dp', None, 'space'), may hold values from -6 to 6
- conv_weight: bfloat16 [2, 9, 640, 320], P('segment'), may hold values from -0.078125 to 0.078125
- ctrl_weight: bfloat16 [2, 320, 320], P('segment'), may hold values from -0.3125 to 0.3125
- norm_gain: float32 [2, 640], P('segment'), may hold values from 0.1 to 1.9
- norm_bias: float32 [2, 640], P('segment'), may hold values from -3 to 3
Outputs:
- acts: bfloat16 [2, 8, 1, 128, 128, 320], P('segment', 'dp', None, 'space')
- grad_conv: bfloat16 [2, 9, 640, 320], P('segment')
- grad_ctrl: float32 [2, 320, 320], P('segment')
- grad_gain: float32 [2, 640], P('segment')
- grad_bias: float32 [2, 640], P('segment')
All inputs are finite; a program needn't handle non-finite values.
Results may differ from a plain program's by a relative error of at most 0.0061.
Values may be sent and summed in bfloat16 or wider, within the bound.
A program may use at most 128 MiB of HBM per device.

v0:
```python
from functools import partial

import jax
import jax.numpy as jnp
from jax import lax
from jax.sharding import PartitionSpec as P

GROUPS = 32


epsilon = 1e-05


def extended(block, sides, width):
    for axis, dim in sides:
        count = lax.axis_size(axis)
        forward = [(i, i + 1) for i in range(count - 1)]
        backward = [(target, source) for source, target in forward]
        low = lax.ppermute(
            lax.slice_in_dim(block, block.shape[dim] - width, None, axis=dim), axis, forward
        )
        high = lax.ppermute(lax.slice_in_dim(block, 0, width, axis=dim), axis, backward)
        block = jnp.concatenate([low, block, high], axis=dim)
    return block


def passed_along(value, axis, steps):
    count = lax.axis_size(axis)
    first, last = (max(0, -steps), min(count, count - steps))
    return lax.ppermute(value, axis, [(source, source + steps) for source in range(first, last)])


def group_sums(values, encoder, channels, groups):
    lead = values.shape[:-1]
    narrow = values[..., :channels].reshape(lead + (groups, channels // groups)).sum(axis=(1, 2, 4))
    wide = values.reshape(lead + (groups, 2 * channels // groups)).sum(axis=(1, 2, 4))
    return jnp.where(encoder, narrow, wide)


def spread(stat, encoder, channels, groups):
    narrow = jnp.repeat(stat, channels // groups, axis=-1)
    narrow = jnp.concatenate([narrow, jnp.zeros_like(narrow)], -1)
    wide = jnp.repeat(stat, 2 * channels // groups, axis=-1)
    return jnp.where(encoder, narrow, wide)[:, None, None, :]


def take_slot(store, slot):
    return lax.dynamic_index_in_dim(store, slot, 0, keepdims=False)


def put_slot(store, slot, value, valid):
    previous = take_slot(store, slot)
    return lax.dynamic_update_index_in_dim(store, jnp.where(valid, value, previous), slot, 0)


def convolve(padded, weight, row_count, col_count):
    width = padded.shape[-1]
    total = jnp.zeros((padded.shape[0] * row_count * col_count, weight.shape[-1]), jnp.float32)
    for tap_id in range(9):
        row_off, col_off = divmod(tap_id, 3)
        piece = padded[:, row_off : row_off + row_count, col_off : col_off + col_count, :].reshape(
            -1, width
        )
        total = total + jnp.dot(piece, weight[tap_id], preferred_element_type=jnp.float32)
    return total.reshape(padded.shape[0], row_count, col_count, -1)


def transpose_conv(source, weight, row_count, col_count):
    channels = source.shape[-1]
    total = jnp.zeros((source.shape[0] * row_count * col_count, weight.shape[1]), jnp.float32)
    for tap_id in range(9):
        row_off, col_off = divmod(tap_id, 3)
        piece = source[
            :, 2 - row_off : 2 - row_off + row_count, 2 - col_off : 2 - col_off + col_count, :
        ].reshape(-1, channels)
        total = total + lax.dot_general(
            piece, weight[tap_id], (((1,), (1,)), ((), ())), preferred_element_type=jnp.float32
        )
    return total.reshape(source.shape[0], row_count, col_count, -1)


def weight_grad(padded, grad_out, row_count, col_count):
    width = padded.shape[-1]
    flat = grad_out.reshape(-1, grad_out.shape[-1])
    parts = []
    for tap_id in range(9):
        row_off, col_off = divmod(tap_id, 3)
        piece = padded[:, row_off : row_off + row_count, col_off : col_off + col_count, :].reshape(
            -1, width
        )
        parts.append(
            lax.dot_general(
                piece, flat, (((0,), (0,)), ((), ())), preferred_element_type=jnp.float32
            )
        )
    return jnp.stack(parts)


def on_device(latents, hint, cotangent, conv_weight, ctrl_weight, norm_gain, norm_bias):
    segments = lax.axis_size("segment")
    halfway = segments // 2
    segment_id = lax.axis_index("segment")
    encoder = segment_id < halfway
    micro_count, frames, row_count, col_count, channels = latents.shape
    wide_ch = 2 * channels
    groups = GROUPS
    height = row_count * lax.axis_size("space")
    weight = conv_weight[0]
    control = ctrl_weight[0]
    gain_vec = norm_gain[0]
    norm_shift = norm_bias[0]
    cell_count = jnp.where(encoder, 1.0, 2.0) * float(height * col_count * (channels // groups))
    channel_mask = jnp.where(encoder, jnp.arange(wide_ch) < channels, True).astype(jnp.float32)
    tick_count = micro_count + segments - 1
    branch_base = jnp.where(encoder, 1, 2).astype(jnp.int32)

    def forward_work(width, padded, hint_one):
        if width == 0:
            return jnp.zeros((frames, row_count, col_count, channels), jnp.float32)
        mixed = convolve(padded[..., :width], weight[:, :width], row_count, col_count)
        ctrl = jnp.dot(hint_one.reshape(-1, channels), control, preferred_element_type=jnp.float32)
        return mixed + ctrl.reshape(mixed.shape)

    forward_branches = [
        partial(forward_work, 0),
        partial(forward_work, channels),
        partial(forward_work, wide_ch),
    ]

    def forward_tick(moment, carry):
        inbox, skips, joined_store, padded_store, mean_store, rstd_store, outputs = carry
        micro_id = moment - segment_id
        valid = (micro_id >= 0) & (micro_id < micro_count)
        slot = jnp.clip(micro_id, 0, micro_count - 1)
        current = jnp.where(segment_id == 0, take_slot(latents, slot), inbox)
        joined = jnp.concatenate([current, take_slot(skips, slot)], -1)
        values = joined.astype(jnp.float32)
        total = lax.psum(group_sums(values, encoder, channels, groups), "space")
        mean_group = total / cell_count
        centered = values - spread(mean_group, encoder, channels, groups)
        squares = lax.psum(group_sums(centered * centered, encoder, channels, groups), "space")
        var_group = squares / cell_count
        rstd_group = lax.rsqrt(var_group + epsilon)
        normed = centered * spread(rstd_group, encoder, channels, groups)
        act = (jax.nn.silu(normed * gain_vec + norm_shift) * channel_mask).astype(jnp.bfloat16)
        padded = extended(act, (("space", 1),), 1)
        padded = jnp.pad(padded, ((0, 0), (0, 0), (1, 1), (0, 0)))
        hint_one = take_slot(hint, slot)
        branch = jnp.where(valid, branch_base, 0)
        mixed = lax.switch(branch, forward_branches, padded, hint_one)
        output = (current.astype(jnp.float32) + mixed).astype(jnp.bfloat16)
        passed = passed_along(output, "segment", 1)
        across = passed_along(output, "segment", halfway)
        source_id = moment - (segment_id - halfway)
        arrived = jnp.logical_not(encoder) & (source_id >= 0) & (source_id < micro_count)
        skips = put_slot(skips, jnp.clip(source_id, 0, micro_count - 1), across, arrived)
        joined_store = put_slot(joined_store, slot, joined, valid)
        padded_store = put_slot(padded_store, slot, padded, valid)
        mean_store = put_slot(mean_store, slot, mean_group, valid)
        rstd_store = put_slot(rstd_store, slot, rstd_group, valid)
        outputs = put_slot(outputs, slot, output, valid)
        return (passed, skips, joined_store, padded_store, mean_store, rstd_store, outputs)

    block_shape = (frames, row_count, col_count, channels)
    start = (
        jnp.zeros(block_shape, jnp.bfloat16),
        jnp.zeros((micro_count,) + block_shape, jnp.bfloat16),
        jnp.zeros((micro_count, frames, row_count, col_count, wide_ch), jnp.bfloat16),
        jnp.zeros((micro_count, frames, row_count + 2, col_count + 2, wide_ch), jnp.bfloat16),
        jnp.zeros((micro_count, frames, groups), jnp.float32),
        jnp.zeros((micro_count, frames, groups), jnp.float32),
        jnp.zeros((micro_count,) + block_shape, jnp.bfloat16),
    )
    forward_state = lax.fori_loop(0, tick_count, forward_tick, start)
    joined_store, padded_store, mean_store, rstd_store, outputs = forward_state[2:]

    def backward_work(width, out_rows, source, padded, hint_one, grad_out, grad_w, grad_ctrl):
        if width == 0:
            return (
                jnp.zeros((frames, out_rows, col_count, wide_ch), jnp.float32),
                grad_w,
                grad_ctrl,
            )
        dact = transpose_conv(source, weight[:, :width], out_rows, col_count)
        if width < wide_ch:
            dact = jnp.pad(dact, ((0, 0), (0, 0), (0, 0), (0, wide_ch - width)))
        taps = weight_grad(padded[..., :width], grad_out, row_count, col_count)
        grad_w = grad_w.at[:, :width].add(taps)
        flat = grad_out.reshape(-1, channels)
        grad_ctrl = grad_ctrl + lax.dot_general(
            hint_one.reshape(-1, channels),
            flat,
            (((0,), (0,)), ((), ())),
            preferred_element_type=jnp.float32,
        )
        return (dact, grad_w, grad_ctrl)

    def backward_tick(moment, carry):
        inbox, skip_grads, grad_w, grad_ctrl, grad_gain, grad_bias = carry
        micro_id = moment - (segments - 1 - segment_id)
        valid = (micro_id >= 0) & (micro_id < micro_count)
        slot = jnp.clip(micro_id, 0, micro_count - 1)
        incoming = jnp.where(segment_id == segments - 1, take_slot(cotangent, slot), inbox)
        summed = (
            incoming.astype(jnp.float32) + take_slot(skip_grads, slot).astype(jnp.float32)
        ).astype(jnp.bfloat16)
        grad_out = jnp.where(encoder, summed, incoming)
        mean_full = spread(take_slot(mean_store, slot), encoder, channels, groups)
        rstd_full = spread(take_slot(rstd_store, slot), encoder, channels, groups)
        normed = (take_slot(joined_store, slot).astype(jnp.float32) - mean_full) * rstd_full
        raised = normed * gain_vec + norm_shift
        padded = take_slot(padded_store, slot)
        hint_one = take_slot(hint, slot)
        branch = jnp.where(valid, branch_base, 0)
        source = extended(grad_out, (("space", 1),), 1)
        source = jnp.pad(source, ((0, 0), (0, 0), (1, 1), (0, 0)))
        branches = [partial(backward_work, width, row_count) for width in (0, channels, wide_ch)]
        dact, grad_w, grad_ctrl = lax.switch(
            branch, branches, source, padded, hint_one, grad_out, grad_w, grad_ctrl
        )
        sigma = jax.nn.sigmoid(raised)
        draised = dact * sigma * (1.0 + raised * (1.0 - sigma)) * channel_mask
        grad_gain = grad_gain + jnp.sum(draised * normed, axis=(0, 1, 2))
        grad_bias = grad_bias + jnp.sum(draised, axis=(0, 1, 2))
        dnormed = draised * gain_vec
        first_sum, second_sum = lax.psum(
            (
                group_sums(dnormed, encoder, channels, groups),
                group_sums(dnormed * normed, encoder, channels, groups),
            ),
            "space",
        )
        first_mean = spread(first_sum / cell_count, encoder, channels, groups)
        second_mean = spread(second_sum / cell_count, encoder, channels, groups)
        djoined = rstd_full * (dnormed - first_mean - normed * second_mean)
        back_grad = (grad_out.astype(jnp.float32) + djoined[..., :channels]).astype(jnp.bfloat16)
        side_grad = jnp.where(encoder, 0.0, djoined[..., channels:]).astype(jnp.bfloat16)
        passed = passed_along(back_grad, "segment", -1)
        across = passed_along(side_grad, "segment", -halfway)
        source_id = moment - (segments - 1 - (segment_id + halfway))
        arrived = encoder & (source_id >= 0) & (source_id < micro_count)
        skip_grads = put_slot(skip_grads, jnp.clip(source_id, 0, micro_count - 1), across, arrived)
        return (passed, skip_grads, grad_w, grad_ctrl, grad_gain, grad_bias)

    back_start = (
        jnp.zeros(block_shape, jnp.bfloat16),
        jnp.zeros((micro_count,) + block_shape, jnp.bfloat16),
        jnp.zeros(weight.shape, jnp.float32),
        jnp.zeros(control.shape, jnp.float32),
        jnp.zeros(gain_vec.shape, jnp.float32),
        jnp.zeros(norm_shift.shape, jnp.float32),
    )
    back_state = lax.fori_loop(0, tick_count, backward_tick, back_start)
    totals = lax.psum((back_state[2], back_state[3], back_state[4], back_state[5]), ("space", "dp"))
    kernel_total = totals[0].astype(jnp.bfloat16)
    ctrl_total, gain_total, bias_total = (totals[1], totals[2], totals[3])
    return (outputs[None], kernel_total[None], ctrl_total[None], gain_total[None], bias_total[None])


def solution(mesh):
    return jax.shard_map(
        on_device,
        mesh=mesh,
        in_specs=(
            P("dp", None, "space", None, None),
            P("dp", None, "space", None, None),
            P("dp", None, "space", None, None),
            P("segment", None, None, None),
            P("segment", None, None),
            P("segment", None),
            P("segment", None),
        ),
        out_specs=(
            P("segment", "dp", None, "space", None, None),
            P("segment", None, None, None),
            P("segment", None, None),
            P("segment", None),
            P("segment", None),
        ),
        check_vma=False,
    )
```

profile of v0, /device:TPU:128, one launch (start us, length us, event | category | flops | bytes accessed | tf_op | source)
XLA Modules:
  0.0 1926.9 jit_solution(11699819585533331840)
XLA Ops:
  7.3 7.8 copy.43
  20.6 535.7 %while.60 = (s32[]{:T(128)}, bf16[1,4,128,320]{2,3,1,0:T(8,128)(2,1)S(1)}, bf16[2,1,4,128,320]{3,4,2,1,0:T(8,128)(2,1)S(1)}, bf16[2,1,4,128,640]{3,4,2,1,0:T(8,1...) while((s32[]{:T(128)}, ...), condition=%wide.region_12.13_spmd.clone.clone, body=%wide.region_0.12_spmd.clone.clone.sunk | while | flops 2019523328 | bytes 100356256 | solution.py:174
  24.0 71.9 %psum.100 = f32[1,32]{1,0:T(1,128)S(1)} all-reduce(f32[1,32]{1,0:T(1,128)S(1)} %fusion.300), channel_id=1, replica_groups=mesh['segment'=2,'space'=32,'dp'=4] {'space'}, use_global_device_ids=true, to_apply=%region_4.4 | all-reduce | flops 32 | bytes 256 | tf_op jit(solution)/shard_map/while/body/eval_jaxpr/psum | solution.py:138
  98.7 69.6 %psum.101 = f32[1,32]{1,0:T(1,128)S(1)} all-reduce(f32[1,32]{1,0:T(1,128)S(1)} %fusion.304), channel_id=1, replica_groups=mesh['segment'=2,'space'=32,'dp'=4] {'space'}, use_global_device_ids=true, to_apply=%region_8.8 | all-reduce | flops 32 | bytes 256 | tf_op jit(solution)/shard_map/while/body/eval_jaxpr/psum | solution.py:141
  185.5 8.2 conditional.9
  204.9 72.2 %psum.100 = f32[1,32]{1,0:T(1,128)S(1)} all-reduce(f32[1,32]{1,0:T(1,128)S(1)} %fusion.300), channel_id=1, replica_groups=mesh['segment'=2,'space'=32,'dp'=4] {'space'}, use_global_device_ids=true, to_apply=%region_4.4 | all-reduce | flops 32 | bytes 256 | tf_op jit(solution)/shard_map/while/body/eval_jaxpr/psum | solution.py:138
  279.8 69.6 %psum.101 = f32[1,32]{1,0:T(1,128)S(1)} all-reduce(f32[1,32]{1,0:T(1,128)S(1)} %fusion.304), channel_id=1, replica_groups=mesh['segment'=2,'space'=32,'dp'=4] {'space'}, use_global_device_ids=true, to_apply=%region_8.8 | all-reduce | flops 32 | bytes 256 | tf_op jit(solution)/shard_map/while/body/eval_jaxpr/psum | solution.py:141
  366.6 8.2 conditional.9
  386.0 72.1 %psum.100 = f32[1,32]{1,0:T(1,128)S(1)} all-reduce(f32[1,32]{1,0:T(1,128)S(1)} %fusion.300), channel_id=1, replica_groups=mesh['segment'=2,'space'=32,'dp'=4] {'space'}, use_global_device_ids=true, to_apply=%region_4.4 | all-reduce | flops 32 | bytes 256 | tf_op jit(solution)/shard_map/while/body/eval_jaxpr/psum | solution.py:138
  460.8 69.6 %psum.101 = f32[1,32]{1,0:T(1,128)S(1)} all-reduce(f32[1,32]{1,0:T(1,128)S(1)} %fusion.304), channel_id=1, replica_groups=mesh['segment'=2,'space'=32,'dp'=4] {'space'}, use_global_device_ids=true, to_apply=%region_8.8 | all-reduce | flops 32 | bytes 256 | tf_op jit(solution)/shard_map/while/body/eval_jaxpr/psum | solution.py:141
  560.9 580.4 %while.61 = (s32[]{:T(128)}, bf16[1,4,128,320]{2,1,3,0:T(4,128)(2,1)S(1)}, bf16[2,1,4,128,320]{3,2,4,1,0:T(4,128)(2,1)S(1)}, f32[9,640,320]{1,2,0:T(8,128)}, f32...) while((s32[]{:T(128)}, ...), condition=%wide.region_29.30_spmd.clone.clone.clone, body=%wide.region_13.29_spmd.clone.clone.clone.sunk | while | flops 3899587328 | bytes 215082864 | solution.py:253
  604.4 20.1 %fusion.317 = (f32[640]{0:T(1024)S(1)}, f32[640]{0:T(1024)S(1)}, f32[1,4,128,640]{2,1,3,0:T(4,128)S(1)}) fusion(f32[640]{0:T(1024)S(1)} %fusion.310, f32[640]{0:T(1024)S(1)} %fusion.312, bf16[1,1,4,128,640]{3,4,2,1,0:T(8,128)(2,1)S(1)} %constant_dynamic-slice_fusion.22, f32[640]{0:T(1024)S(1)} %fusion.313, ...), kind=kLoop, calls=%fused_computation.353.clone.1 | loop fusion | flops 5569280 | bytes 3294720 | tf_op jit(solution)/shard_map/while/body/eval_jaxpr/reduce_sum | solution.py:224
  624.6 9.2 fusion.318
  634.8 10.7 fusion.319
  648.6 74.5 %all-reduce.12 = (f32[1,32]{1,0:T(1,128)S(1)}, f32[1,32]{1,0:T(1,128)S(1)}) all-reduce(f32[1,32]{1,0:T(1,128)S(1)} %fusion.320, f32[1,32]{1,0:T(1,128)S(1)} %fusion.321), channel_id=1, replica_groups=mesh['segment'=2,'space'=32,'dp'=4] {'space'}, use_global_device_ids=true, to_apply=%region_26.26 | all-reduce | flops 64 | bytes 512 | tf_op jit(solution)/shard_map/while/body/eval_jaxpr/psum | solution.py:226
  723.8 6.2 fusion.323
  733.2 9.3 collective-permute-done.6
  763.2 49.9 %conditional.10 = (f32[1,4,128,640]{2,1,3,0:T(4,128)}, f32[9,640,320]{1,2,0:T(8,128)}, f32[320,320]{1,0:T(8,128)}) conditional(s32[]{:T(128)} %clamp.28, (f32[9,640,320]{1,2,0:T(8,128)}, f32[320,320]{1,0:T(8,128)}) %tuple.223, (bf16[1,6,130,320]{2,1,3,0:T(8,128)(2,1)S(1)}, bf16[9,640,320]{2,1,0:T(8,128)(2,1)}, ...), branch_computations={%region_14.14_spmd, %region_15.15_spmd, %region_16.16_spmd} | conditional | flops 3884298240 | bytes 178470176 | solution.py:218
  773.7 23.3 %scatter-add.0 = f32[9,640,320]{1,2,0:T(8,128)} dynamic-update-slice(f32[9,640,320]{1,2,0:T(8,128)} %get-tuple-element.1073, f32[9,320,320]{1,2,0:T(8,128)} %slice_add_fusion, s32[]{:T(128)} %constant.280.clone, s32[]{:T(128)} %constant.280.clone, s32[]{:T(128)} %constant.280.clone) | dynamic-update-slice | bytes 7372804 | tf_op jit(solution)/shard_map/while/body/eval_jaxpr/cond/branch_1_fun/scatter-add | solution.py:188
  813.2 20.1 %fusion.317 = (f32[640]{0:T(1024)S(1)}, f32[640]{0:T(1024)S(1)}, f32[1,4,128,640]{2,1,3,0:T(4,128)S(1)}) fusion(f32[640]{0:T(1024)S(1)} %fusion.310, f32[640]{0:T(1024)S(1)} %fusion.312, bf16[1,1,4,128,640]{3,4,2,1,0:T(8,128)(2,1)S(1)} %constant_dynamic-slice_fusion.22, f32[640]{0:T(1024)S(1)} %fusion.313, ...), kind=kLoop, calls=%fused_computation.353.clone.1 | loop fusion | flops 5569280 | bytes 3294720 | tf_op jit(solution)/shard_map/while/body/eval_jaxpr/reduce_sum | solution.py:224
  833.3 9.2 fusion.318
  843.5 10.7 fusion.319
  857.3 73.0 %all-reduce.12 = (f32[1,32]{1,0:T(1,128)S(1)}, f32[1,32]{1,0:T(1,128)S(1)}) all-reduce(f32[1,32]{1,0:T(1,128)S(1)} %fusion.320, f32[1,32]{1,0:T(1,128)S(1)} %fusion.321), channel_id=1, replica_groups=mesh['segment'=2,'space'=32,'dp'=4] {'space'}, use_global_device_ids=true, to_apply=%region_26.26 | all-reduce | flops 64 | bytes 512 | tf_op jit(solution)/shard_map/while/body/eval_jaxpr/psum | solution.py:226
  931.1 6.2 fusion.323
  961.9 49.9 %conditional.10 = (f32[1,4,128,640]{2,1,3,0:T(4,128)}, f32[9,640,320]{1,2,0:T(8,128)}, f32[320,320]{1,0:T(8,128)}) conditional(s32[]{:T(128)} %clamp.28, (f32[9,640,320]{1,2,0:T(8,128)}, f32[320,320]{1,0:T(8,128)}) %tuple.223, (bf16[1,6,130,320]{2,1,3,0:T(8,128)(2,1)S(1)}, bf16[9,640,320]{2,1,0:T(8,128)(2,1)}, ...), branch_computations={%region_14.14_spmd, %region_15.15_spmd, %region_16.16_spmd} | conditional | flops 3884298240 | bytes 178470176 | solution.py:218
  972.4 23.3 %scatter-add.0 = f32[9,640,320]{1,2,0:T(8,128)} dynamic-update-slice(f32[9,640,320]{1,2,0:T(8,128)} %get-tuple-element.1073, f32[9,320,320]{1,2,0:T(8,128)} %slice_add_fusion, s32[]{:T(128)} %constant.280.clone, s32[]{:T(128)} %constant.280.clone, s32[]{:T(128)} %constant.280.clone) | dynamic-update-slice | bytes 7372804 | tf_op jit(solution)/shard_map/while/body/eval_jaxpr/cond/branch_1_fun/scatter-add | solution.py:188
  1011.8 20.1 %fusion.317 = (f32[640]{0:T(1024)S(1)}, f32[640]{0:T(1024)S(1)}, f32[1,4,128,640]{2,1,3,0:T(4,128)S(1)}) fusion(f32[640]{0:T(1024)S(1)} %fusion.310, f32[640]{0:T(1024)S(1)} %fusion.312, bf16[1,1,4,128,640]{3,4,2,1,0:T(8,128)(2,1)S(1)} %constant_dynamic-slice_fusion.22, f32[640]{0:T(1024)S(1)} %fusion.313, ...), kind=kLoop, calls=%fused_computation.353.clone.1 | loop fusion | flops 5569280 | bytes 3294720 | tf_op jit(solution)/shard_map/while/body/eval_jaxpr/reduce_sum | solution.py:224
  1032.0 9.2 fusion.318
  1042.2 10.7 fusion.319
  1056.0 73.0 %all-reduce.12 = (f32[1,32]{1,0:T(1,128)S(1)}, f32[1,32]{1,0:T(1,128)S(1)}) all-reduce(f32[1,32]{1,0:T(1,128)S(1)} %fusion.320, f32[1,32]{1,0:T(1,128)S(1)} %fusion.321), channel_id=1, replica_groups=mesh['segment'=2,'space'=32,'dp'=4] {'space'}, use_global_device_ids=true, to_apply=%region_26.26 | all-reduce | flops 64 | bytes 512 | tf_op jit(solution)/shard_map/while/body/eval_jaxpr/psum | solution.py:226
  1129.7 6.2 fusion.323
  1141.3 776.5 %all-reduce.17 = (bf16[9,640,320]{1,2,0:T(8,128)(2,1)}, f32[1,640]{1,0:T(1,128)}, f32[1,640]{1,0:T(1,128)}) all-reduce(f32[9,640,320]{1,2,0:T(8,128)} %get-tuple-element.1131, f32[1,640]{1,0:T(1,128)S(1)} %broadcast_in_dim.225, f32[1,640]{1,0:T(1,128)S(1)} %broadcast_in_dim.226), channel_id=1, replica_groups=mesh['segment'=2,'space'=32,'dp'=4] {'space','dp'}, use_global_device_ids=true, to_apply=%region_30.31 | all-reduce | flops 1844480 | bytes 11069440 | tf_op jit(solution)/shard_map/psum | solution.py:254
  (525 shorter events, 265.5 us)
Async XLA Ops:
  7.2 1910.6 %all-reduce.16.cloned.1.call-start = ((), (), s32[]{:S(2)}) async-start(), calls=%async_computation | async-start | bytes 983040 | tf_op jit(solution)/shard_map/psum | solution.py:254
  168.8 9.3 copy-start.26
  170.0 14.5 copy-start.4
  170.1 11.7 collective-permute-start
  174.0 10.5 collective-permute-start.1
  195.9 5.4 collective-permute-start.2
  349.8 9.3 copy-start.26
  351.1 14.5 copy-start.4
  351.1 11.6 collective-permute-start
  355.1 10.5 collective-permute-start.1
  376.9 5.4 collective-permute-start.2
  530.9 9.3 copy-start.26
  532.2 14.5 copy-start.4
  532.2 11.6 collective-permute-start
  536.1 10.5 collective-permute-start.1
  550.7 5.4 collective-permute-start.2
  585.4 14.6 collective-permute-start.3
  589.9 10.6 collective-permute-start.4
  723.8 18.6 copy-start.16
  730.1 12.4 copy-start.23
  730.3 12.2 collective-permute-start.6
  731.9 12.1 collective-permute-start.5
  746.4 14.1 collective-permute-start.3
  748.4 12.1 collective-permute-start.4
  931.1 10.1 copy-start.16
  937.5 3.7 collective-permute-start.6
  939.1 3.5 collective-permute-start.5
  945.1 14.1 collective-permute-start.3
  947.1 12.1 collective-permute-start.4
  1129.7 10.1 copy-start.16
  1136.1 3.7 collective-permute-start.6
  1137.8 3.5 collective-permute-start.5
  (42 other events, 139.2 us)
Sparse Core Ops, SparseCore 0:
  1141.4 212.4 all-reduce.15
where the time goes:
time: 1940 us; the launch traced here: 1930 us
  blocking collectives  1420 us (73%)
  other arithmetic  210 us (11%)
  local copies, waits for them, and re-layouts  139 us (7%)
  starting transfers between devices  48 us (2%)
  matrix products  45.1 us (2%)
  loops' own time  24.5 us (1%)
  waiting for transfers between devices  23.5 us (1%)
    psum x1, blocking collectives, on_device(): lax.psum((back_state[2], back_state[3], back_state[4], back_state[5]), ('...  776 us
    psum x3, blocking collectives, backward_tick(): lax.psum((group_sums(dnormed, encoder, channels, groups), group_sums(dnor...  220 us
    psum x3, blocking collectives, forward_tick(): total = lax.psum(group_sums(values, encoder, channels, groups), 'space')  216 us
    psum x3, blocking collectives, forward_tick(): lax.psum(group_sums(centered * centered, encoder, channels, groups), 'spa...  209 us
    reduce_sum x18, other arithmetic, group_sums(): values.reshape(lead + (groups, 2 * channels // groups)).sum(axis=(1, 2, 4))  66.9 us
    reduce_sum x3, other arithmetic, backward_tick(): grad_bias = grad_bias + jnp.sum(draised, axis=(0, 1, 2))  60.4 us
    scatter-add x2, local copies, waits for them, and re-layouts, backward_work(): grad_w = grad_w.at[:, :width].add(taps)  46.6 us
  transfers between devices with their start and end apart: 22, of which 10 were waited for; matrix products, arithmetic and copies ran while one was open for 3% of the time, Pallas kernels for 0%

commit v1 on v0

v1 whole, which is shorter than its diff:
```python
import functools

import jax
import jax.numpy as jnp
from jax import lax
from jax.experimental import pallas as pl
from jax.experimental.pallas import tpu as pltpu
from jax.sharding import PartitionSpec as P

MESH = pl.DeviceIdType.MESH
F32 = jnp.float32
BF16 = jnp.bfloat16
EPS = 1e-05
GROUPS = 32
PART = 2048
ROW = 128
CHUNK = 32


def nt_dot(a, b):
    return lax.dot_general(a, b, (((1,), (1,)), ((), ())), preferred_element_type=F32)


def tn_dot(a, b):
    return lax.dot_general(a, b, (((0,), (0,)), ((), ())), preferred_element_type=F32)


def nn_dot(a, b):
    return jnp.dot(a, b, preferred_element_type=F32)


def fold(v):
    return v.reshape(v.shape[0] // 8, 8, v.shape[1]).sum(axis=0)


def sigmoid(v):
    return 1.0 / (1.0 + jnp.exp(-v))


class Slots:
    def __init__(self):
        self.index = {}

    def __call__(self, name):
        return self.index.setdefault(name, len(self.index))


def body(
    dims,
    slots,
    lat_hbm, hint_hbm, cot_hbm, w_hbm, cw_hbm, gain_ref, bias_ref,
    acts_hbm, conv_out, ctrl_out, gain_out, bias_out,
    x_ext, g_ext, hint_v, w_v, cw_v, act, y, dact, shifted, out_v,
    s_send, s_recv, stat_v, grads, r1, r2, r3, s1, s2, gathered, zeros_v, ctrl_v,
    send_sem, recv_sem, local_sem,
):
    NZ, NX, NY, samples, rows, channels = dims
    cells = rows * ROW
    ext = cells + 2 * ROW
    space_count = NZ * NX
    seg = lax.axis_index("segment")
    space = lax.axis_index("space")
    dp = lax.axis_index("dp")
    zi = space // NX
    xi = lax.rem(space, NX)
    other = 1 - seg
    up = lax.rem(space + space_count - 1, space_count)
    down = lax.rem(space + 1, space_count)
    size = {"x": NX, "y": NY, "z": NZ}
    mine = {"x": xi, "y": dp, "z": zi}

    def peer(axis, k, core=None):
        if axis == "x":
            place = {"space": zi * NX + lax.rem(xi + k, NX), "dp": dp}
        elif axis == "z":
            place = {"space": lax.rem(zi + k, NZ) * NX + xi, "dp": dp}
        else:
            place = {"space": space, "dp": lax.rem(dp + k, NY)}
        place["segment"] = seg if core is None else core
        return place

    def at(space_id, core):
        return {"space": space_id, "dp": dp, "segment": core}

    def send(name, src, dst, place):
        slot = slots(name)
        return pltpu.make_async_remote_copy(
            src_ref=src, dst_ref=dst, send_sem=send_sem.at[slot], recv_sem=recv_sem.at[slot],
            device_id=(place["segment"], place["space"], place["dp"]), device_id_type=MESH,
        )

    def local(name, src, dst):
        return pltpu.make_async_copy(src, dst, local_sem.at[slots("local " + name)])

    inner = pl.ds(ROW, cells)
    low, high = pl.ds(0, ROW), pl.ds(ROW + cells, ROW)
    first, last = pl.ds(ROW, ROW), pl.ds(cells, ROW)
    kernel_rows = 9 * channels

    def loads(is_encoder):
        table = {
            "hint": (hint_hbm, hint_v),
            "weight": (w_hbm, w_v),
            "control": (cw_hbm, cw_v),
        }
        if is_encoder:
            table["main"] = (lat_hbm, x_ext.at[:, inner, :])
        else:
            table["main"] = (cot_hbm, g_ext.at[:, inner, :])
        return {key: functools.partial(local, key, *pair) for key, pair in table.items()}

    @pl.when(seg == 0)
    def _():
        for key in ("main", "control", "hint", "weight"):
            loads(True)[key]().start()

    @pl.when(seg == 1)
    def _():
        for key in ("main", "hint", "weight", "control"):
            loads(False)[key]().start()

    barrier = pltpu.get_barrier_semaphore()
    places = [peer("x", k) for k in range(1, NX)]
    places += [peer("y", k) for k in range(1, NY)]
    places += [peer("z", k) for k in range(1, NZ)]
    places += [peer("z", k, other) for k in range(NZ)]
    places += [at(n, c) for n in (up, down) for c in (seg, other)]
    for place in places:
        pl.semaphore_signal(
            barrier, inc=1,
            device_id=(place["segment"], place["space"], place["dp"]), device_id_type=MESH,
        )
    pl.semaphore_wait(barrier, len(places))

    lane = lax.broadcasted_iota(jnp.int32, (channels, channels), 0).astype(F32)
    lane_t = lax.broadcasted_iota(jnp.int32, (channels, channels), 1).astype(F32)

    def group_mean(values, width):
        same = jnp.floor((lane + 0.5) / width) == jnp.floor((lane_t + 0.5) / width)
        return jnp.dot(
            values, jnp.where(same, 1.0, 0.0),
            precision=lax.Precision.HIGHEST, preferred_element_type=F32,
        ) / width

    def edges(halo_name, ref, src, core):
        return [
            send(halo_name + " down", src[1], ref.at[:, low, :], at(down, core)),
            send(halo_name + " up", src[0], ref.at[:, high, :], at(up, core)),
        ]

    def zero_outside(ref):
        blank = jnp.zeros((samples, ROW, channels), ref.dtype)

        @pl.when(space == 0)
        def _():
            ref[:, 0:ROW, :] = blank

        @pl.when(space == space_count - 1)
        def _():
            ref[:, ROW + cells:ext, :] = blank

    def local_stats(ref, base, name):
        for b in range(samples):
            def add(i, total):
                v = ref[b, pl.ds(pl.multiple_of(base + i * CHUNK, CHUNK), CHUNK), :].astype(F32)
                return total + fold(v)
            total = lax.fori_loop(0, cells // CHUNK, add, jnp.zeros((8, channels), F32))
            mean = total.sum(axis=0, keepdims=True) / cells

            def square(i, total):
                v = ref[b, pl.ds(pl.multiple_of(base + i * CHUNK, CHUNK), CHUNK), :].astype(F32) - mean
                return total + fold(v * v)
            spread = lax.fori_loop(0, cells // CHUNK, square, jnp.zeros((8, channels), F32))
            s_send[slots.buffer(name), b:b + 1, :] = mean
            s_send[slots.buffer(name), samples + b:samples + b + 1, :] = spread.sum(axis=0, keepdims=True)

    def exchange(name, axis, core=None, own=True):
        src = s_send.at[slots.buffer(name)]
        copies = []
        for k in range(0 if core is not None else 1, size[axis]):
            label = f"{name} {k}"
            copies.append(send(label, src, s_recv.at[slots.inbox(label)], peer(axis, k, core)))
        return copies

    def arrivals(name, axis, own):
        out = []
        if own:
            out.append(s_send.at[slots.buffer(name)])
        for k in range(1 if own else 0, size[axis]):
            out.append(s_recv.at[slots.inbox(f"{name} {k}")])
        return out

    def merge(refs, count):
        mean = sum(r[0:samples, :] for r in refs) / len(refs)
        spread = sum(r[samples:2 * samples, :] for r in refs)
        apart = sum(jnp.square(r[0:samples, :] - mean) for r in refs)
        return mean, spread + count * apart

    def finish_stats(mean, spread, width):
        total = cells * space_count
        padded = jnp.concatenate([mean, jnp.zeros((8 - samples, channels), F32)], axis=0)
        middle = group_mean(padded, width)
        offset = padded - middle
        both = jnp.concatenate([spread, jnp.zeros((8 - samples, channels), F32)], axis=0)
        var = group_mean(both / total + offset * offset, width)
        stat_v[0] = middle
        stat_v[1] = lax.rsqrt(var + EPS)

    def small_sum(name, axes, value):
        for axis in axes:
            step = f"{name} {axis}"
            s_send[slots.buffer(step)] = value
            copies = exchange(step, axis)
            for c in copies:
                c.start()
            for c in copies:
                c.wait()
            value = sum(r[...] for r in arrivals(step, axis, True))
        return value

    def activate(halves):
        for b in range(samples):
            middle = stat_v[0, b:b + 1, :]
            scale = stat_v[1, b:b + 1, :]

            def step(i, carry):
                where = pl.ds(pl.multiple_of(i * CHUNK, CHUNK), CHUNK)
                xhat = (x_ext[b, where, :].astype(F32) - middle) * scale
                for h in halves:
                    u = xhat * gain_ref[h:h + 1, :] + bias_ref[h:h + 1, :]
                    act[h, b, where, :] = (u * sigmoid(u)).astype(BF16)
                return carry
            lax.fori_loop(0, ext // CHUNK, step, 0)
        for h in halves:
            zero_outside(act.at[h])

    def column_mask(shape, column):
        return lax.broadcasted_iota(jnp.int32, shape, 0) != column

    def shift(v, step):
        column = 0 if step == 1 else ROW - 1
        moved = pltpu.roll(v, step % ROW, axis=0)
        return jnp.where(column_mask(v.shape, column), moved, 0.0)

    BLOCK = 2 * ROW

    def forward(halves):
        def step(i, carry):
            b = i // (cells // BLOCK)
            start = pl.multiple_of(lax.rem(i, cells // BLOCK) * BLOCK, BLOCK)
            for dc in range(3):
                total = None
                if dc == 1:
                    total = nn_dot(hint_v[b, pl.ds(start, BLOCK), :], cw_v[...])
                for dr in range(3):
                    for h in halves:
                        lhs = act[h, b, pl.ds(start + dr * ROW, BLOCK), :]
                        part = nn_dot(lhs, w_v[3 * dr + dc, channels * h:channels * (h + 1), :])
                        total = part if total is None else total + part
                y[dc] = total
            for r in range(BLOCK // ROW):
                where = pl.ds(r * ROW, ROW)
                total = y[1, where, :] + shift(y[0, where, :], 1) + shift(y[2, where, :], -1)
                x = x_ext[b, pl.ds(start + (r + 1) * ROW, ROW), :].astype(F32)
                out_v[b, pl.ds(start + r * ROW, ROW), :] = (x + total).astype(BF16)
            return carry
        lax.fori_loop(0, samples * cells // BLOCK, step, 0)

    def transposed(halves):
        def step(i, carry):
            b = i // (cells // BLOCK)
            start = pl.multiple_of(lax.rem(i, cells // BLOCK) * BLOCK, BLOCK)
            for h in halves:
                for dc in range(3):
                    total = None
                    for dr in range(3):
                        lhs = g_ext[b, pl.ds(start + (2 - dr) * ROW, BLOCK), :]
                        part = nt_dot(lhs, w_v[3 * dr + dc, channels * h:channels * (h + 1), :])
                        total = part if total is None else total + part
                    y[dc] = total
                for r in range(BLOCK // ROW):
                    where = pl.ds(r * ROW, ROW)
                    total = y[1, where, :] + shift(y[0, where, :], -1) + shift(y[2, where, :], 1)
                    dact[h, b, pl.ds(start + r * ROW, ROW), :] = total
            return carry
        lax.fori_loop(0, samples * cells // BLOCK, step, 0)

    def shift_gradient():
        def step(i, carry):
            b = i // rows
            start = pl.multiple_of(lax.rem(i, rows) * ROW, ROW)
            g = g_ext[b, pl.ds(start + ROW, ROW), :].astype(F32)
            shifted[0, b, pl.ds(start, ROW), :] = shift(g, -1).astype(BF16)
            shifted[1, b, pl.ds(start, ROW), :] = shift(g, 1).astype(BF16)
            return carry
        lax.fori_loop(0, samples * rows, step, 0)

    def control_gradient(offset):
        total = sum(tn_dot(hint_v[b], g_ext[b, inner, :]) for b in range(samples))
        grads[offset:offset + channels, :] = total.astype(BF16)

    def kernel_gradient(halves, row):
        width = channels * len(halves)
        for h in halves:
            for dc in range(3):
                total = None
                for b in range(samples):
                    g = g_ext[b, inner, :] if dc == 1 else shifted[dc // 2, b]
                    lhs = act[h, b, row * ROW:row * ROW + cells, :]
                    part = tn_dot(lhs, g)
                    total = part if total is None else total + part
                base = (3 * row + dc) * width + h * channels
                grads[base:base + channels, :] = total.astype(BF16)

    def norm_backward(halves):
        lines = []
        for b in range(samples):
            middle = stat_v[0, b:b + 1, :]
            scale = stat_v[1, b:b + 1, :]

            def step(i, sums):
                where = pl.ds(pl.multiple_of(i * CHUNK, CHUNK), CHUNK)
                outer = pl.ds(pl.multiple_of(i * CHUNK + ROW, CHUNK), CHUNK)
                xhat = (x_ext[b, outer, :].astype(F32) - middle) * scale
                out = []
                for n, h in enumerate(halves):
                    u = xhat * gain_ref[h:h + 1, :] + bias_ref[h:h + 1, :]
                    s = sigmoid(u)
                    du = dact[h, b, where, :] * s * (1.0 + u * (1.0 - s))
                    dact[h, b, where, :] = du
                    out.append(sums[2 * n] + fold(du))
                    out.append(sums[2 * n + 1] + fold(du * xhat))
                return tuple(out)
            start = tuple(jnp.zeros((8, channels), F32) for _ in range(2 * len(halves)))
            sums = lax.fori_loop(0, cells // CHUNK, step, start)
            lines.append([s.sum(axis=0, keepdims=True) for s in sums])
        order = []
        for n in range(len(halves)):
            order += [lines[b][2 * n] for b in range(samples)]
            order += [lines[b][2 * n + 1] for b in range(samples)]
        for n in range(len(order), 8):
            order.append(jnp.zeros((1, channels), F32))
        return jnp.concatenate(order, axis=0)

    def part_geometry(p):
        return ORDERS[p], part_rows(size, p)

    stride = tuple(max(part_rows(size, p)[stage] for p in range(3)) for stage in range(3))

    def scatter_copies(p, stage):
        axes, ns = part_geometry(p)
        axis, n = axes[stage], ns[stage]
        src = (grads, s1, s2)[stage]
        dst = (r1, r2, r3)[stage]
        base = p * PART if stage == 0 else p * stride[stage - 1]
        copies = []
        for k in range(1, size[axis]):
            to = lax.rem(mine[axis] + k, size[axis])
            where = pl.ds(pl.multiple_of(base + to * n, 16), n)
            inbox = dst.at[p, pl.ds((k - 1) * n, n), :]
            copies.append(send(f"rs {p} {stage} {k}", src.at[where, :], inbox, peer(axis, k)))
        return copies

    def final_offset(p):
        axes, ns = part_geometry(p)
        return p * PART + sum(mine[a] * n for a, n in zip(axes, ns))

    def scatter_sum(p, stage):
        axes, ns = part_geometry(p)
        axis, n = axes[stage], ns[stage]
        src = (grads, s1, s2)[stage]
        inbox = (r1, r2, r3)[stage]
        base = p * PART if stage == 0 else p * stride[stage - 1]
        own = base + mine[axis] * n
        if stage == 0:
            dst, to = s1, p * stride[0]
        elif stage == 1:
            dst, to = s2, p * stride[1]
        else:
            dst, to = gathered, final_offset(p)
        chunk = 16

        def step(i, carry):
            total = src[pl.ds(pl.multiple_of(own + i * chunk, 16), chunk), :].astype(F32)
            for k in range(size[axis] - 1):
                total += inbox[p, pl.ds(pl.multiple_of(k * n + i * chunk, 16), chunk), :].astype(F32)
            dst[pl.ds(pl.multiple_of(to + i * chunk, 16), chunk), :] = total.astype(BF16)
            return carry
        lax.fori_loop(0, n // chunk, step, 0)

    def gather_copies(p, stage):
        axes, ns = part_geometry(p)
        axis, n = axes[stage], ns[stage]
        offset = p * PART + sum(mine[a] * m for a, m in zip(axes[:stage + 1], ns[:stage + 1]))
        where = pl.ds(pl.multiple_of(offset, 16), n)
        return [
            send(f"ag {p} {stage} {k}", gathered.at[where, :], gathered.at[where, :], peer(axis, k))
            for k in range(1, size[axis])
        ]

    def gather_wait(p, stage):
        axes, ns = part_geometry(p)
        axis, n = axes[stage], ns[stage]
        base = p * PART + sum(mine[a] * m for a, m in zip(axes[:stage], ns[:stage]))
        for k in range(1, size[axis]):
            source = lax.rem(mine[axis] + size[axis] - k, size[axis])
            where = pl.ds(pl.multiple_of(base + source * n, 16), n)
            send(f"ag {p} {stage} {k}", gathered.at[where, :], gathered.at[where, :], peer(axis, k)).wait()

    def start(copies):
        for c in copies:
            c.start()

    def wait(copies):
        for c in copies:
            c.wait()

    def reduce_rest(parts):
        for stage in range(3):
            for p in parts:
                wait(scatter_copies(p, stage))
                scatter_sum(p, stage)
                start(scatter_copies(p, stage + 1) if stage < 2 else gather_copies(p, 2))
        for stage in (2, 1, 0):
            for p in parts:
                gather_wait(p, stage)
                if stage > 0:
                    start(gather_copies(p, stage - 1))

    def finish(parts, halves, base):
        width = channels * len(halves)
        copies = []
        if len(halves) == 1:
            for tap in range(9):
                copies.append(local(f"out {tap}", gathered.at[pl.ds(tap * width, width), :], conv_out.at[tap, pl.ds(0, width), :]))
                copies.append(local(f"zero {tap}", zeros_v, conv_out.at[tap, pl.ds(width, channels), :]))
        else:
            for tap in range(9):
                copies.append(local(f"out {tap}", gathered.at[pl.ds(tap * width, width), :], conv_out.at[tap]))
        start(copies)

        ctrl_out[...] = gathered[base:base + channels, :].astype(F32)
        wait(copies)

    @pl.when(seg == 0)
    def _encoder():
        halves = (0,)
        load = loads(True)
        load["main"]().wait()
        halo = edges("lat", x_ext, (x_ext.at[:, first, :], x_ext.at[:, last, :]), 0)
        start(halo)
        local_stats(x_ext, ROW, "a x")
        copies = exchange("a x", "x")
        start(copies)
        wait(copies)
        mean, spread = merge(arrivals("a x", "x", True), float(cells))
        s_send[slots.buffer("a z"), 0:samples, :] = mean
        s_send[slots.buffer("a z"), samples:2 * samples, :] = spread
        copies = exchange("a z", "z")
        start(copies)
        wait(copies)
        mean, spread = merge(arrivals("a z", "z", True), float(cells * NX))
        finish_stats(mean, spread, channels // GROUPS)
        wait(halo)
        activate(halves)
        for key in ("hint", "weight", "control"):
            load[key]().wait()
        forward(halves)
        ahead = [send("o", out_v, x_ext.at[:, inner, :], at(space, 1))]
        ahead += edges("o", x_ext, (out_v.at[:, pl.ds(0, ROW), :], out_v.at[:, pl.ds(cells - ROW, ROW), :]), 1)
        save = local("acts", out_v, acts_hbm)
        start(ahead)
        save.start()
        local_stats(out_v, 0, "b x")
        copies = exchange("b x", "x")
        start(copies)
        wait(copies)
        mean, spread = merge(arrivals("b x", "x", True), float(cells))
        s_send[slots.buffer("b z"), 0:samples, :] = mean
        s_send[slots.buffer("b z"), samples:2 * samples, :] = spread
        stats = exchange("b z", "z", core=1)
        start(stats)
        for c in ahead + stats:
            c.wait_send()
        save.wait()
        back = [send("g", out_v, g_ext.at[:, inner, :], at(space, 0))]
        back += edges("g", g_ext, (out_v.at[:, pl.ds(0, ROW), :], out_v.at[:, pl.ds(cells - ROW, ROW), :]), 0)
        for c in back:
            c.wait_recv()
        zero_outside(g_ext)
        shift_gradient()
        for row in range(3):
            kernel_gradient(halves, row)
        control_gradient(kernel_rows)
        grads[kernel_rows + channels:2 * PART, :] = jnp.zeros((2 * PART - kernel_rows - channels, channels), BF16)
        for p in (0, 1):
            start(scatter_copies(p, 0))
        transposed(halves)
        sums = norm_backward(halves)
        sums = small_sum("e", ("x", "z", "y"), sums)
        blank = jnp.zeros((1, channels), F32)
        bias_out[0:1, :] = sums[0:samples].sum(axis=0, keepdims=True)
        gain_out[0:1, :] = sums[samples:2 * samples].sum(axis=0, keepdims=True)
        bias_out[1:2, :] = blank
        gain_out[1:2, :] = blank
        zeros_v[...] = jnp.zeros(zeros_v.shape, BF16)
        reduce_rest((0, 1))
        finish((0, 1), halves, kernel_rows)

    @pl.when(seg == 1)
    def _decoder():
        halves = (0, 1)
        load = loads(False)
        load["main"]().wait()
        halo = edges("cot", g_ext, (g_ext.at[:, first, :], g_ext.at[:, last, :]), 1)
        start(halo)
        load["hint"]().wait()
        control_gradient(2 * kernel_rows)
        grads[2 * kernel_rows + channels:3 * PART, :] = jnp.zeros((3 * PART - 2 * kernel_rows - channels, channels), BF16)
        shift_gradient()
        load["weight"]().wait()
        load["control"]().wait()
        wait(halo)
        zero_outside(g_ext)
        transposed(halves)
        ahead = [send("o", out_v, x_ext.at[:, inner, :], at(space, 1))]
        ahead += edges("o", x_ext, (out_v.at[:, pl.ds(0, ROW), :], out_v.at[:, pl.ds(cells - ROW, ROW), :]), 1)
        stats = exchange("b z", "z", core=1)
        for c in ahead + stats:
            c.wait_recv()
        mean, spread = merge(arrivals("b z", "z", False), float(cells * NX))
        finish_stats(mean, spread, 2 * channels // GROUPS)
        sums = norm_backward(halves)
        sums = small_sum("c", ("x", "z"), sums)
        total = float(cells * space_count)
        width = 2 * channels // GROUPS
        for h in halves:
            gain = gain_ref[h:h + 1, :]
            stat_v[2 + h] = group_mean(sums * gain, width) / total
        for b in range(samples):
            middle = stat_v[0, b:b + 1, :]
            scale = stat_v[1, b:b + 1, :]

            def step(i, carry):
                where = pl.ds(pl.multiple_of(i * CHUNK, CHUNK), CHUNK)
                outer = pl.ds(pl.multiple_of(i * CHUNK + ROW, CHUNK), CHUNK)
                xhat = (x_ext[b, outer, :].astype(F32) - middle) * scale
                dj = []
                for h in halves:
                    m1 = stat_v[2 + h, 4 * h + b:4 * h + b + 1, :]
                    m2 = stat_v[2 + h, 4 * h + 2 + b:4 * h + 3 + b, :]
                    dx = dact[h, b, where, :] * gain_ref[h:h + 1, :]
                    dj.append((dx - m1 - xhat * m2) * scale)
                dh = (g_ext[b, outer, :].astype(F32) + dj[0]).astype(BF16)
                dskip = dj[1].astype(BF16)
                out_v[b, where, :] = (dh.astype(F32) + dskip.astype(F32)).astype(BF16)
                return carry
            lax.fori_loop(0, cells // CHUNK, step, 0)
        back = [send("g", out_v, g_ext.at[:, inner, :], at(space, 0))]
        back += edges("g", g_ext, (out_v.at[:, pl.ds(0, ROW), :], out_v.at[:, pl.ds(cells - ROW, ROW), :]), 0)
        start(back)
        activate(halves)
        for row in range(3):
            kernel_gradient(halves, row)
        for p in (0, 1, 2):
            start(scatter_copies(p, 0))
        for c in back:
            c.wait_send()
        forward(halves)
        save = local("acts", out_v, acts_hbm)
        save.start()
        sums = small_sum("f", ("y",), sums)
        for h in halves:
            bias_out[h:h + 1, :] = sums[4 * h:4 * h + 2].sum(axis=0, keepdims=True)
            gain_out[h:h + 1, :] = sums[4 * h + 2:4 * h + 4].sum(axis=0, keepdims=True)
        reduce_rest((0, 1, 2))
        finish((0, 1, 2), halves, 2 * kernel_rows)
        save.wait()


ORDERS = (("x", "y", "z"), ("y", "x", "z"), ("z", "x", "y"))


def part_rows(size, p):
    rows, out = PART, []
    for axis in ORDERS[p]:
        rows //= size[axis]
        out.append(rows)
    return tuple(out)


class Names(Slots):
    def __init__(self):
        super().__init__()
        self.buffers = Slots()
        self.inboxes = Slots()

    def buffer(self, name):
        return self.buffers(name)

    def inbox(self, name):
        return self.inboxes(name)


def on_device(grid, latents, hint, cotangent, conv_weight, ctrl_weight, norm_gain, norm_bias):
    NZ, NX, NY = grid
    samples, frames, rows, cols, channels = latents.shape
    cells = rows * cols
    ext = cells + 2 * ROW
    dims = (NZ, NX, NY, samples, rows, channels)
    flat = lambda a: a.reshape(samples, cells, channels)
    vmem = pl.BlockSpec(memory_space=pltpu.VMEM)
    anywhere = pl.BlockSpec(memory_space=pl.ANY)
    size = {"x": NX, "y": NY, "z": NZ}
    stride = [max(part_rows(size, p)[stage] for p in range(3)) for stage in range(3)]
    inbox = [max(part_rows(size, p)[stage] * (size[ORDERS[p][stage]] - 1) for p in range(3)) for stage in range(3)]
    out = pl.pallas_call(
        functools.partial(body, dims, Names()),
        out_shape=(
            jax.ShapeDtypeStruct((samples, cells, channels), BF16),
            jax.ShapeDtypeStruct((9, 2 * channels, channels), BF16),
            jax.ShapeDtypeStruct((channels, channels), F32),
            jax.ShapeDtypeStruct((2, channels), F32),
            jax.ShapeDtypeStruct((2, channels), F32),
        ),
        in_specs=[anywhere] * 5 + [vmem] * 2,
        out_specs=(anywhere, anywhere, vmem, vmem, vmem),
        scratch_shapes=[
            pltpu.VMEM((samples, ext, channels), BF16),
            pltpu.VMEM((samples, ext, channels), BF16),
            pltpu.VMEM((samples, cells, channels), BF16),
            pltpu.VMEM((9, 2 * channels, channels), BF16),
            pltpu.VMEM((channels, channels), BF16),
            pltpu.VMEM((2, samples, ext, channels), BF16),
            pltpu.VMEM((3, 2 * ROW, channels), F32),
            pltpu.VMEM((2, samples, cells, channels), F32),
            pltpu.VMEM((2, samples, cells, channels), BF16),
            pltpu.VMEM((samples, cells, channels), BF16),
            pltpu.VMEM((12, 8, channels), F32),
            pltpu.VMEM((64, 8, channels), F32),
            pltpu.VMEM((4, 8, channels), F32),
            pltpu.VMEM((3 * PART, channels), BF16),
            pltpu.VMEM((3, inbox[0], channels), BF16),
            pltpu.VMEM((3, inbox[1], channels), BF16),
            pltpu.VMEM((3, inbox[2], channels), BF16),
            pltpu.VMEM((3 * stride[0], channels), BF16),
            pltpu.VMEM((3 * stride[1], channels), BF16),
            pltpu.VMEM((3 * PART, channels), BF16),
            pltpu.VMEM((channels, channels), BF16),
            pltpu.VMEM((channels, channels), F32),
            pltpu.SemaphoreType.DMA((160,)),
            pltpu.SemaphoreType.DMA((160,)),
            pltpu.SemaphoreType.DMA((200,)),
        ],
        compiler_params=pltpu.CompilerParams(
            collective_id=0, has_side_effects=True, vmem_limit_bytes=60 * 1024 * 1024
        ),
    )(
        flat(latents), flat(hint), flat(cotangent), conv_weight[0], ctrl_weight[0],
        norm_gain.reshape(2, channels), norm_bias.reshape(2, channels),
    )
    acts, conv, ctrl, gain, bias = out
    return (
        acts.reshape((1,) + latents.shape),
        conv[None],
        ctrl[None],
        gain.reshape(1, 2 * channels),
        bias.reshape(1, 2 * channels),
    )


def grid_of(mesh):
    space = mesh.shape["space"]
    columns = 4 if space >= 32 else 2
    return (space // columns, columns, mesh.shape["dp"])


def solution(mesh):
    return jax.shard_map(
        functools.partial(on_device, grid_of(mesh)),
        mesh=mesh,
        in_specs=(
            P("dp", None, "space", None, None),
            P("dp", None, "space", None, None),
            P("dp", None, "space", None, None),
            P("segment", None, None, None),
            P("segment", None, None),
            P("segment", None),
            P("segment", None),
        ),
        out_specs=(
            P("segment", "dp", None, "space", None, None),
            P("segment", None, None, None),
            P("segment", None, None),
            P("segment", None),
            P("segment", None),
        ),
        check_vma=False,
    )
```

time: 1940 us -> 170 us (0.09)
  the two profiles are of different devices: /device:TPU:128 before, /device:TPU:32 now
where the time goes in v1:
time: 170 us; the launch traced here: 169 us
  Pallas kernels  139 us (82%)
  local copies, waits for them, and re-layouts  28 us (16%)
    pallas_call x1, Pallas kernels, on_device(): pl.pallas_call(functools.partial(body, dims, Names()), out_shape=(jax.Sha...  139 us
    unnamed x13, local copies, waits for them, and re-layouts  25.4 us

profile of v1, /device:TPU:32, one launch (start us, length us, event | category | flops | bytes accessed | tf_op | source)
XLA Modules:
  0.0 169.0 jit_solution(1230429215799579397)
XLA Ops:
  0.6 0.7 reduce
  1.3 0.7 reshape.37.gain_ref
  2.0 0.7 reduce.1
  2.7 0.7 reshape.38.bias_ref
  3.3 2.2 %copy.12 = bf16[2,1,4,128,320]{4,3,2,0,1:T(8,128)(2,1)} copy(bf16[2,1,4,128,320]{3,4,2,1,0:T(8,128)(2,1)} %param.7) | data formatting | bytes 1310720 | tf_op args[0]
  5.6 2.3 %copy.13 = bf16[2,1,4,128,320]{4,3,2,0,1:T(8,128)(2,1)} copy(bf16[2,1,4,128,320]{3,4,2,1,0:T(8,128)(2,1)} %param.8) | data formatting | bytes 1310720 | tf_op args[1]
  7.9 2.2 %copy.14 = bf16[2,1,4,128,320]{4,3,2,0,1:T(8,128)(2,1)} copy(bf16[2,1,4,128,320]{3,4,2,1,0:T(8,128)(2,1)} %param.9) | data formatting | bytes 1310720 | tf_op args[2]
  10.2 7.7 %copy.15 = bf16[1,9,640,320]{3,2,1,0:T(8,128)(2,1)} copy(bf16[1,9,640,320]{2,3,1,0:T(8,128)(2,1)} %param.10) | data formatting | bytes 7372800 | tf_op args[3]
  17.9 138.9 %shard_map.110 = (bf16[2,512,320]{2,1,0:T(8,128)(2,1)}, bf16[9,640,320]{2,1,0:T(8,128)(2,1)}, f32[320,320]{1,0:T(8,128)}, f32[2,320]{1,0:T(2,128)}, f32[2,320]{1,0:T(2,128)}) custom-call(bf16[2,512,320]{2,1,0:T(8,128)(2,1)} %bitcast.10, bf16[2,512,320]{2,1,0:T(8,128)(2,1)} %bitcast.11, bf16[2,512,320]{2,1,0:T(8,128)(2,1)} %bitcast.12, ...), custom_call_target="tpu_custom_call" | custom-call | tf_op jit(solution)/shard_map/pallas_call | solution.py:617
  156.8 0.0 copy-start.2
  156.8 0.0 copy-start.1
  156.8 0.0 copy-start
  156.8 2.3 %copy.16 = bf16[1,2,1,4,128,320]{4,5,3,2,1,0:T(8,128)(2,1)} copy(bf16[1,2,1,4,128,320]{5,4,3,1,2,0:T(8,128)(2,1)} %bitcast.13) | data formatting | bytes 1310720
  159.1 7.7 %copy.17 = bf16[1,9,640,320]{2,3,1,0:T(8,128)(2,1)} copy(bf16[1,9,640,320]{3,2,1,0:T(8,128)(2,1)} %bitcast.9) | data formatting | bytes 7372800
  166.9 0.0 copy-done.2
  166.9 0.7 reshape.40
  167.5 0.0 copy-done.1
  167.5 0.7 reshape.41
  168.2 0.0 copy-done
  168.2 0.8 copy.19
Async XLA Ops:
  156.8 10.1 %copy-start.2 = (f32[2,320]{1,0:T(2,128)S(1)}, f32[2,320]{1,0:T(2,128)}, u32[]{:S(2)}) copy-start(f32[2,320]{1,0:T(2,128)} %get-tuple-element.13) | copy-start | bytes 7684
  156.8 10.7 %copy-start.1 = (f32[2,320]{1,0:T(2,128)S(1)}, f32[2,320]{1,0:T(2,128)}, u32[]{:S(2)}) copy-start(f32[2,320]{1,0:T(2,128)} %get-tuple-element.14) | copy-start | bytes 7684
  156.8 11.4 %copy-start = (f32[320,320]{1,0:T(8,128)S(1)}, f32[320,320]{1,0:T(8,128)}, u32[]{:S(2)}) copy-start(f32[320,320]{1,0:T(8,128)} %get-tuple-element.12) | copy-start | bytes 1228804

commit v2 on v1

v2 whole, which is shorter than its diff:
```python
import functools

import jax
import jax.numpy as jnp
from jax import lax
from jax.experimental import pallas as pl
from jax.experimental.pallas import tpu as pltpu
from jax.sharding import PartitionSpec as P

MESH = pl.DeviceIdType.MESH
F32 = jnp.float32
BF16 = jnp.bfloat16
EPS = 1e-05
GROUPS = 32
LANES = 128
UNIT = 2048
CHUNK = 32
HIGH = lax.Precision.HIGHEST

ORDERS = (("x", "y", "z"), ("y", "x", "z"), ("z", "x", "y"))
PARTS = {1: ((0, 2 * UNIT), (1, 2 * UNIT), (2, UNIT)), 2: ((0, 3 * UNIT), (1, 3 * UNIT), (2, 2 * UNIT))}


def nt_dot(a, b, precision=None):
    return lax.dot_general(
        a, b, (((1,), (1,)), ((), ())), precision=precision, preferred_element_type=F32
    )


def tn_dot(a, b, precision=None):
    return lax.dot_general(
        a, b, (((0,), (0,)), ((), ())), precision=precision, preferred_element_type=F32
    )


def nn_dot(a, b):
    return jnp.dot(a, b, preferred_element_type=F32)


def sigmoid(v):
    return 1.0 / (1.0 + jnp.exp(-v))


def part_rows(size, halves, p):
    rows, out = PARTS[halves][p][1], []
    for axis in ORDERS[PARTS[halves][p][0]]:
        rows //= size[axis]
        out.append(rows)
    return tuple(out)


def largest(size, value):
    return [
        max(value(part_rows(size, halves, p), ORDERS[PARTS[halves][p][0]], stage) for halves in (1, 2) for p in range(3))
        for stage in range(3)
    ]


class Slots:
    def __init__(self):
        self.index = {}

    def __call__(self, name):
        return self.index.setdefault(name, len(self.index))


class Names(Slots):
    def __init__(self):
        super().__init__()
        self.local = Slots()
        self.boxes = {}

    def box(self, name, count):
        return self.boxes.setdefault(name, (sum(n for _, n in self.boxes.values()), count))[0]


def body(
    dims,
    slots,
    lat_hbm, hint_hbm, cot_hbm, w_hbm, cw_hbm, gain_ref, bias_ref,
    acts_hbm, grads_hbm, gain_out, bias_out,
    x_ext, g_ext, hint_v, w_v, cw_v, wb, act, act_t, g3, y, dact, out_v, last_v,
    columns, sums_v, gain_c, bias_c,
    s_recv, grads, r1, r2, r3, s1, s2, gathered,
    send_sem, recv_sem, local_sem,
):
    NZ, NX, NY, samples, rows, channels = dims
    cells = rows * LANES
    wide = samples * LANES
    space_count = NZ * NX
    seg = lax.axis_index("segment")
    space = lax.axis_index("space")
    dp = lax.axis_index("dp")
    zi = space // NX
    xi = lax.rem(space, NX)
    other = 1 - seg
    up = lax.rem(space + space_count - 1, space_count)
    down = lax.rem(space + 1, space_count)
    size = {"x": NX, "y": NY, "z": NZ}
    mine = {"x": xi, "y": dp, "z": zi}

    def peer(axis, k, core=None):
        if axis == "x":
            place = {"space": zi * NX + lax.rem(xi + k, NX), "dp": dp}
        elif axis == "z":
            place = {"space": lax.rem(zi + k, NZ) * NX + xi, "dp": dp}
        else:
            place = {"space": space, "dp": lax.rem(dp + k, NY)}
        place["segment"] = seg if core is None else core
        return place

    def at(space_id, core):
        return {"space": space_id, "dp": dp, "segment": core}

    def send(name, src, dst, place):
        slot = slots(name)
        return pltpu.make_async_remote_copy(
            src_ref=src, dst_ref=dst, send_sem=send_sem.at[slot], recv_sem=recv_sem.at[slot],
            device_id=(place["segment"], place["space"], place["dp"]), device_id_type=MESH,
        )

    def local(name, src, dst):
        return pltpu.make_async_copy(src, dst, local_sem.at[slots.local(name)])

    def start(copies):
        for c in copies:
            c.start()

    def wait(copies):
        for c in copies:
            c.wait()

    inner = pl.ds(1, rows)

    def sample(b):
        return pl.ds(b * LANES, LANES)

    def loads(is_encoder, key):
        if key == "weight":
            return [local(key, w_hbm, w_v)]
        if key == "control":
            return [local(key, cw_hbm, cw_v)]
        if key == "hint":
            return [local(f"{key} {b}", hint_hbm.at[b], hint_v.at[:, :, sample(b)]) for b in range(samples)]
        source, target = (lat_hbm, x_ext) if is_encoder else (cot_hbm, g_ext)
        return [local(f"{key} {b}", source.at[b], target.at[inner, :, sample(b)]) for b in range(samples)]

    @pl.when(seg == 0)
    def _():
        for key in ("main", "weight", "control", "hint"):
            start(loads(True, key))

    @pl.when(seg == 1)
    def _():
        for key in ("main", "weight", "hint", "control"):
            start(loads(False, key))

    barrier = pltpu.get_barrier_semaphore()
    places = [peer("x", k) for k in range(1, NX)]
    places += [peer("y", k) for k in range(1, NY)]
    places += [peer("z", k) for k in range(1, NZ)]
    places += [peer("z", k, other) for k in range(NZ)]
    places += [at(n, c) for n in (up, down) for c in (seg, other)]
    for place in places:
        pl.semaphore_signal(
            barrier, inc=1,
            device_id=(place["segment"], place["space"], place["dp"]), device_id_type=MESH,
        )

    line = lax.broadcasted_iota(jnp.int32, (8, LANES), 0)
    ones = jnp.ones((8, LANES), F32)
    first_lane = jnp.where(lax.broadcasted_iota(jnp.int32, (8, LANES), 1) == 0, 1.0, 0.0)

    def to_row(block, pick=None):
        return nt_dot(ones if pick is None else pick, block, HIGH)[0:1, :]

    def to_column(value, k):
        return tn_dot(value, jnp.where(line == k, 1.0, 0.0), HIGH)

    def eight(parts):
        count = sum(p.shape[0] for p in parts)
        if count < 8:
            parts = parts + [jnp.zeros((8 - count, parts[0].shape[1]), F32)]
        return jnp.concatenate(parts, axis=0)

    gain_c[...] = to_column(eight([gain_ref[...]]), 0)
    bias_c[...] = to_column(eight([bias_ref[...]]), 0)

    lane = lax.broadcasted_iota(jnp.int32, (channels, channels), 0).astype(F32)
    lane_t = lax.broadcasted_iota(jnp.int32, (channels, channels), 1).astype(F32)

    def group_mean(values, width):
        same = jnp.floor((lane + 0.5) / width) == jnp.floor((lane_t + 0.5) / width)
        return jnp.dot(
            values, jnp.where(same, 1.0, 0.0), precision=HIGH, preferred_element_type=F32
        ) / width

    def edges(name, ref, src, core):
        return [
            send(name + " down", src[1], ref.at[0], at(down, core)),
            send(name + " up", src[0], ref.at[rows + 1], at(up, core)),
        ]

    def zero_outside(ref):
        blank = jnp.zeros(ref.shape[1:], ref.dtype)

        @pl.when(space == 0)
        def _():
            ref[0] = blank

        @pl.when(space == space_count - 1)
        def _():
            ref[rows + 1] = blank

    def chunks(step, width=CHUNK):
        def run(i, carry):
            step(pl.multiple_of(i * width, width))
            return carry
        lax.fori_loop(0, channels // width, run, 0)

    def local_stats(ref, base, name):
        def step(at_row):
            where = pl.ds(at_row, CHUNK)
            for b in range(samples):
                v = [ref[base + r, where, sample(b)].astype(F32) for r in range(rows)]
                mean = jnp.sum(sum(v), axis=1, keepdims=True) / cells
                sums_v[b, where, :] = jnp.broadcast_to(mean, (CHUNK, LANES))
                sums_v[samples + b, where, :] = sum(jnp.square(t - mean) for t in v)
        chunks(step)
        lines = [to_row(sums_v[b], first_lane) for b in range(samples)]
        lines += [to_row(sums_v[samples + b]) for b in range(samples)]
        put(name, "x", eight(lines))

    def put(name, axis, value):
        s_recv[slots.box(name, size[axis]) + mine[axis]] = value

    def exchange(name, axis, core=None, landing=False):
        base = slots.box(name, size[axis])
        copies = []
        for k in range(0 if core is not None else 1, size[axis]):
            owner = lax.rem(mine[axis] + size[axis] - k, size[axis]) if landing else mine[axis]
            copies.append(send(f"{name} {k}", s_recv.at[base + mine[axis]], s_recv.at[base + owner], peer(axis, k, core)))
        return copies

    def arrivals(name, axis):
        base = slots.box(name, size[axis])
        return [s_recv.at[base + k] for k in range(size[axis])]

    def small_wait(name, axis):
        wait(exchange(name, axis, landing=True))

    def merge(refs, count):
        mean = sum(r[0:samples, :] for r in refs) / len(refs)
        spread = sum(r[samples:2 * samples, :] for r in refs)
        apart = sum(jnp.square(r[0:samples, :] - mean) for r in refs)
        return mean, spread + count * apart

    def finish_stats(mean, spread, width):
        total = cells * space_count
        padded = eight([mean])
        middle = group_mean(padded, width)
        offset = padded - middle
        var = group_mean(eight([spread]) / total + offset * offset, width)
        scale = lax.rsqrt(var + EPS)
        for b in range(samples):
            columns[b] = to_column(middle, b)
            columns[samples + b] = to_column(scale, b)

    def activate(halves):
        for h in halves:
            def step(at_row):
                where = pl.ds(at_row, CHUNK)
                inside = pl.ds(pl.multiple_of(at_row + h * channels, CHUNK), CHUNK)
                gain, bias = gain_c[inside, :], bias_c[inside, :]
                for b in range(samples):
                    middle, rate = columns[b, where, :], columns[samples + b, where, :]
                    for r in range(rows + 2):
                        xhat = (x_ext[r, where, sample(b)].astype(F32) - middle) * rate
                        u = xhat * gain + bias
                        a = (u * sigmoid(u)).astype(BF16)
                        act[r, inside, sample(b)] = a
                        act_t[inside, pl.ds(r * wide + b * LANES, LANES)] = a
            chunks(step)
        blank = jnp.zeros((2 * channels, wide), BF16)
        for r, edge in ((0, 0), (rows + 1, space_count - 1)):
            @pl.when(space == edge)
            def _():
                act[r] = blank
                act_t[:, r * wide:(r + 1) * wide] = blank

    lanes = lax.broadcasted_iota(jnp.int32, (channels, LANES), 1)

    def shift(v, step):
        column = 0 if step == 1 else LANES - 1
        return jnp.where(lanes[:v.shape[0]] != column, pltpu.roll(v, step % LANES, axis=1), 0.0)

    def forward(halves, target):
        width = channels * len(halves)

        def step(r, carry):
            total = None
            for dr in range(3):
                part = nn_dot(w_v[dr, :, 0:width], act[r + dr, 0:width, :])
                total = part if total is None else total + part
            y[0:3 * channels, :] = total
            y[3 * channels:4 * channels, :] = tn_dot(cw_v[...], hint_v[r])
            for b in range(samples):
                def tap(dc):
                    return y[dc * channels:(dc + 1) * channels, sample(b)]
                total = tap(1) + tap(3) + shift(tap(0), 1) + shift(tap(2), -1)
                x = x_ext[r + 1, :, sample(b)].astype(F32)
                target[r, :, sample(b)] = (x + total).astype(BF16)
            return carry
        lax.fori_loop(0, rows, step, 0)

    def turn_weights(halves):
        count = -(-channels * len(halves) // LANES)
        for dc in range(3):
            def block(j, carry):
                where = pl.ds(pl.multiple_of(j * LANES, LANES), LANES)
                taps = [w_v[2 - d, dc * channels:(dc + 1) * channels, where] for d in range(3)]
                wb[dc, where, :] = jnp.concatenate(taps, axis=0).T
                return carry
            lax.fori_loop(0, count, block, 0)

    def transposed(halves):
        def step(r, carry):
            g = g_ext[pl.ds(r, 3)].reshape(3 * channels, wide)
            for h in halves:
                for dc in range(3):
                    y[dc * channels:(dc + 1) * channels, :] = nn_dot(wb[dc, h * channels:(h + 1) * channels, :], g)
                for b in range(samples):
                    def tap(dc):
                        return y[dc * channels:(dc + 1) * channels, sample(b)]
                    dact[h, r, :, sample(b)] = tap(1) + shift(tap(0), -1) + shift(tap(2), 1)
            return carry
        lax.fori_loop(0, rows, step, 0)

    def shift_gradient():
        def step(r, carry):
            for b in range(samples):
                g = g_ext[r + 1, :, sample(b)]
                where = pl.ds(pl.multiple_of(r * wide + b * LANES, LANES), LANES)
                v = g.astype(F32)
                g3[0:channels, where] = shift(v, -1).astype(BF16)
                g3[channels:2 * channels, where] = g
                g3[2 * channels:3 * channels, where] = shift(v, 1).astype(BF16)
            return carry
        lax.fori_loop(0, rows, step, 0)

    def blocks(value, base):
        count = value.shape[0]
        for j in range(value.shape[1] // LANES):
            grads[base + j * count:base + (j + 1) * count, :] = value[:, j * LANES:(j + 1) * LANES].astype(BF16)

    def control_gradient(base):
        total = None
        for r in range(rows):
            where = pl.ds(r * wide, wide)
            part = nt_dot(hint_v[r], g3[channels:2 * channels, where])
            total = part if total is None else total + part
        blocks(jnp.concatenate([total, jnp.zeros((channels, 3 * LANES - channels), F32)], axis=1), base)

    def kernel_gradient(halves, dr):
        width = 3 * LANES if len(halves) == 1 else 2 * channels
        total = nt_dot(g3[...], act_t[0:width, dr * wide:(dr + rows) * wide])
        blocks(total, dr * 3 * channels * (width // LANES))

    def norm_backward(halves):
        for h in halves:
            def step(at_row):
                where = pl.ds(at_row, CHUNK)
                inside = pl.ds(pl.multiple_of(at_row + h * channels, CHUNK), CHUNK)
                gain, bias = gain_c[inside, :], bias_c[inside, :]
                for b in range(samples):
                    middle, rate = columns[b, where, :], columns[samples + b, where, :]
                    first = second = None
                    for r in range(rows):
                        xhat = (x_ext[r + 1, where, sample(b)].astype(F32) - middle) * rate
                        u = xhat * gain + bias
                        s = sigmoid(u)
                        du = dact[h, r, where, sample(b)] * s * (1.0 + u * (1.0 - s))
                        dact[h, r, where, sample(b)] = du
                        first = du if first is None else first + du
                        second = du * xhat if second is None else second + du * xhat
                    sums_v[4 * h + b, where, :] = first
                    sums_v[4 * h + samples + b, where, :] = second
            chunks(step)
        return eight([to_row(sums_v[k]) for k in range(4 * len(halves))])

    stride = tuple(largest(size, lambda ns, axes, stage: ns[stage]))

    def part_geometry(p, halves):
        parts = PARTS[halves]
        base = sum(n for _, n in parts[:p])
        return ORDERS[parts[p][0]], part_rows(size, halves, p), base

    def stage_base(p, halves, stage):
        base = part_geometry(p, halves)[2]
        return base if stage == 0 else p * stride[stage - 1]

    def scatter_copies(p, halves, stage):
        axes, ns, _ = part_geometry(p, halves)
        axis, n = axes[stage], ns[stage]
        src = (grads, s1, s2)[stage]
        dst = (r1, r2, r3)[stage]
        base = stage_base(p, halves, stage)
        copies = []
        for k in range(1, size[axis]):
            to = lax.rem(mine[axis] + k, size[axis])
            where = pl.ds(pl.multiple_of(base + to * n, 16), n)
            inbox = dst.at[p, pl.ds((k - 1) * n, n), :]
            copies.append(send(f"rs {p} {stage} {k}", src.at[where, :], inbox, peer(axis, k)))
        return copies

    def scatter_sum(p, halves, stage):
        axes, ns, part_base = part_geometry(p, halves)
        axis, n = axes[stage], ns[stage]
        src = (grads, s1, s2)[stage]
        inbox = (r1, r2, r3)[stage]
        own = stage_base(p, halves, stage) + mine[axis] * n
        if stage == 0:
            dst, to = s1, p * stride[0]
        elif stage == 1:
            dst, to = s2, p * stride[1]
        else:
            dst, to = gathered, part_base + sum(mine[a] * m for a, m in zip(axes, ns))
        chunk = 64 if n % 64 == 0 else 16

        def step(i, carry):
            total = src[pl.ds(pl.multiple_of(own + i * chunk, 16), chunk), :].astype(F32)
            for k in range(size[axis] - 1):
                total += inbox[p, pl.ds(pl.multiple_of(k * n + i * chunk, 16), chunk), :].astype(F32)
            dst[pl.ds(pl.multiple_of(to + i * chunk, 16), chunk), :] = total.astype(BF16)
            return carry
        lax.fori_loop(0, n // chunk, step, 0)

    def gather_copies(p, halves, stage):
        axes, ns, part_base = part_geometry(p, halves)
        axis, n = axes[stage], ns[stage]
        offset = part_base + sum(mine[a] * m for a, m in zip(axes[:stage + 1], ns[:stage + 1]))
        where = pl.ds(pl.multiple_of(offset, 16), n)
        return [
            send(f"ag {p} {stage} {k}", gathered.at[where, :], gathered.at[where, :], peer(axis, k))
            for k in range(1, size[axis])
        ]

    def gather_wait(p, halves, stage):
        axes, ns, part_base = part_geometry(p, halves)
        axis, n = axes[stage], ns[stage]
        base = part_base + sum(mine[a] * m for a, m in zip(axes[:stage], ns[:stage]))
        for k in range(1, size[axis]):
            source = lax.rem(mine[axis] + size[axis] - k, size[axis])
            where = pl.ds(pl.multiple_of(base + source * n, 16), n)
            send(f"ag {p} {stage} {k}", gathered.at[where, :], gathered.at[where, :], peer(axis, k)).wait()

    def reduce_rest(halves, name, axes, value):
        def small_start(stage):
            put(f"{name} {stage}", axes[stage], value)
            start(exchange(f"{name} {stage}", axes[stage]))

        small_start(0)
        for stage in range(3):
            for p in range(3):
                wait(scatter_copies(p, halves, stage))
                scatter_sum(p, halves, stage)
                start(scatter_copies(p, halves, stage + 1) if stage < 2 else gather_copies(p, halves, 2))
            if stage < len(axes):
                small_wait(f"{name} {stage}", axes[stage])
                value = sum(r[...] for r in arrivals(f"{name} {stage}", axes[stage]))
                if stage + 1 < len(axes):
                    small_start(stage + 1)
        for stage in (2, 1, 0):
            for p in range(3):
                gather_wait(p, halves, stage)
                if stage > 0:
                    start(gather_copies(p, halves, stage - 1))
                else:
                    start([part_out(p, halves)])
        return value

    def part_out(p, halves):
        base, n = part_geometry(p, halves)[2], PARTS[halves][p][1]
        return local(f"part {p}", gathered.at[pl.ds(base, n), :], grads_hbm.at[pl.ds(base, n), :])

    def saves(source):
        return [local(f"acts {b}", source.at[:, :, sample(b)], acts_hbm.at[b]) for b in range(samples)]

    def clear_tail(halves):
        used = 3 * 3 * channels * (3 if halves == 1 else 5) + 3 * channels
        total = sum(n for _, n in PARTS[halves])
        grads[used:total, :] = jnp.zeros((total - used, LANES), BF16)

    @pl.when(seg == 0)
    def _():
        wait(loads(True, "main"))
        local_stats(x_ext, 1, "a x")

    @pl.when(seg == 1)
    def _():
        wait(loads(False, "main"))
        clear_tail(2)
        shift_gradient()

    pl.semaphore_wait(barrier, len(places))

    @pl.when(seg == 0)
    def _encoder():
        halves = (0,)
        start(exchange("a x", "x"))
        halo = edges("lat", x_ext, (x_ext.at[1], x_ext.at[rows]), 0)
        start(halo)
        act_t[channels:3 * LANES, :] = jnp.zeros((3 * LANES - channels, act_t.shape[1]), BF16)
        clear_tail(1)
        small_wait("a x", "x")
        mean, spread = merge(arrivals("a x", "x"), float(cells))
        put("a z", "z", eight([mean, spread]))
        start(exchange("a z", "z"))
        wait(loads(True, "weight"))
        turn_weights(halves)
        small_wait("a z", "z")
        mean, spread = merge(arrivals("a z", "z"), float(cells * NX))
        finish_stats(mean, spread, channels // GROUPS)
        wait(halo)
        activate(halves)
        wait(loads(True, "hint"))
        wait(loads(True, "control"))
        forward(halves, out_v)
        ahead = [send("o", out_v, x_ext.at[inner], at(space, 1))]
        start(ahead)
        start(saves(out_v))
        local_stats(out_v, 0, "b x")
        start(exchange("b x", "x"))
        small_wait("b x", "x")
        mean, spread = merge(arrivals("b x", "x"), float(cells))
        put("b z", "z", eight([mean, spread]))
        stats = exchange("b z", "z", core=1)
        start(stats)
        halo = edges("o", x_ext, (out_v.at[0], out_v.at[rows - 1]), 1)
        start(halo)
        ahead += halo
        for c in ahead + stats:
            c.wait_send()
        wait(saves(out_v))
        send("g", out_v, g_ext.at[inner], at(space, 0)).wait_recv()
        shift_gradient()
        kernel_gradient(halves, 0)
        kernel_gradient(halves, 1)
        start(scatter_copies(0, 1, 0))
        kernel_gradient(halves, 2)
        start(scatter_copies(1, 1, 0))
        control_gradient(3 * 3 * channels * 3)
        start(scatter_copies(2, 1, 0))
        for c in edges("g", g_ext, (out_v.at[0], out_v.at[rows - 1]), 0):
            c.wait_recv()
        zero_outside(g_ext)
        transposed(halves)
        sums = norm_backward(halves)
        sums = reduce_rest(1, "e", ("x", "z", "y"), sums)
        blank = jnp.zeros((1, channels), F32)
        bias_out[...] = jnp.concatenate([sums[0:1] + sums[1:2], blank], axis=1)
        gain_out[...] = jnp.concatenate([sums[2:3] + sums[3:4], blank], axis=1)
        wait([part_out(p, len(halves)) for p in range(3)])

    @pl.when(seg == 1)
    def _decoder():
        halves = (0, 1)
        halo = edges("cot", g_ext, (g_ext.at[1], g_ext.at[rows]), 1)
        start(halo)
        wait(loads(False, "weight"))
        turn_weights(halves)
        wait(halo)
        zero_outside(g_ext)
        transposed(halves)
        wait(loads(False, "hint"))
        control_gradient(3 * 3 * channels * 5)
        wait(loads(False, "control"))
        send("o", out_v, x_ext.at[inner], at(space, 1)).wait_recv()
        for c in exchange("b z", "z", core=1, landing=True):
            c.wait_recv()
        mean, spread = merge(arrivals("b z", "z"), float(cells * NX))
        width = 2 * channels // GROUPS
        finish_stats(mean, spread, width)
        sums = norm_backward(halves)
        put("c x", "x", sums)
        start(exchange("c x", "x"))
        for c in edges("o", x_ext, (out_v.at[0], out_v.at[rows - 1]), 1):
            c.wait_recv()
        activate(halves)
        small_wait("c x", "x")
        sums = sum(r[...] for r in arrivals("c x", "x"))
        put("c z", "z", sums)
        start(exchange("c z", "z"))
        for dr in range(3):
            kernel_gradient(halves, dr)
        start(scatter_copies(1, 2, 0))
        small_wait("c z", "z")
        start(scatter_copies(2, 2, 0))
        sums = sum(r[...] for r in arrivals("c z", "z"))
        total = float(cells * space_count)
        for h in halves:
            gain = gain_ref[:, h * channels:(h + 1) * channels]
            means = group_mean(sums * gain, width) / total
            for k in range(4):
                columns[4 + 4 * h + k] = to_column(means, 4 * h + k)

        def step(at_row):
            where = pl.ds(at_row, CHUNK)
            gains = [gain_c[pl.ds(pl.multiple_of(at_row + h * channels, CHUNK), CHUNK), :] for h in halves]
            for b in range(samples):
                middle, rate = columns[b, where, :], columns[samples + b, where, :]
                means = [(columns[4 + 4 * h + b, where, :], columns[6 + 4 * h + b, where, :]) for h in halves]
                for r in range(rows):
                    xhat = (x_ext[r + 1, where, sample(b)].astype(F32) - middle) * rate
                    dj = []
                    for h in halves:
                        dx = dact[h, r, where, sample(b)] * gains[h]
                        dj.append((dx - means[h][0] - xhat * means[h][1]) * rate)
                    dh = (g_ext[r + 1, where, sample(b)].astype(F32) + dj[0]).astype(BF16)
                    dskip = dj[1].astype(BF16)
                    out_v[r, where, sample(b)] = (dh.astype(F32) + dskip.astype(F32)).astype(BF16)
        chunks(step)
        back = [send("g", out_v, g_ext.at[inner], at(space, 0))]
        back += edges("g", g_ext, (out_v.at[0], out_v.at[rows - 1]), 0)
        start(back)
        start(scatter_copies(0, 2, 0))
        forward(halves, last_v)
        start(saves(last_v))
        sums = reduce_rest(2, "f", ("y",), sums)
        bias_out[...] = jnp.concatenate([sums[0:1] + sums[1:2], sums[4:5] + sums[5:6]], axis=1)
        gain_out[...] = jnp.concatenate([sums[2:3] + sums[3:4], sums[6:7] + sums[7:8]], axis=1)
        wait([part_out(p, len(halves)) for p in range(3)])
        wait(saves(last_v))
        for c in back:
            c.wait_send()


def deliver(
    channels, acts_in, grads_in, gain_in, bias_in,
    acts_out, conv_out, ctrl_out, gain_out, bias_out, zeros_v, sem,
):
    seg = lax.axis_index("segment")
    high = 3 * channels

    def copies(count):
        out = [
            pltpu.make_async_copy(acts_in, acts_out, sem.at[0]),
        ]
        for dr in range(3):
            for j in range(5):
                target = conv_out.at[pl.ds(dr * high, high), pl.ds(j * LANES, LANES)]
                source = grads_in.at[pl.ds((dr * count + j) * high, high), :] if j < count else zeros_v
                out.append(pltpu.make_async_copy(source, target, sem.at[1 + 5 * dr + j]))
        return out

    def run(count):
        moves = copies(count)
        for c in moves:
            c.start()
        gain_out[...] = gain_in[...]
        bias_out[...] = bias_in[...]
        base, last = 3 * count * high, channels - 2 * LANES
        ctrl_out[:, 0:LANES] = grads_in[base:base + channels, :].astype(F32)
        ctrl_out[:, LANES:2 * LANES] = grads_in[base + channels:base + 2 * channels, :].astype(F32)
        ctrl_out[:, 2 * LANES:channels] = grads_in[base + 2 * channels:base + high, 0:last].astype(F32)
        for c in moves:
            c.wait()

    @pl.when(seg == 0)
    def _():
        zeros_v[...] = jnp.zeros(zeros_v.shape, BF16)
        run(3)

    @pl.when(seg == 1)
    def _():
        run(5)


def on_device(grid, latents, hint, cotangent, conv_weight, ctrl_weight, norm_gain, norm_bias):
    NZ, NX, NY = grid
    samples, frames, rows, cols, channels = latents.shape
    cells = rows * cols
    wide = samples * cols
    dims = (NZ, NX, NY, samples, rows, channels)
    turned = lambda a: a.transpose(0, 1, 2, 4, 3).reshape(samples, rows, channels, cols)
    vmem = pl.BlockSpec(memory_space=pltpu.VMEM)
    anywhere = pl.BlockSpec(memory_space=pl.ANY)
    size = {"x": NX, "y": NY, "z": NZ}
    stride = largest(size, lambda ns, axes, stage: ns[stage])
    inbox = largest(size, lambda ns, axes, stage: ns[stage] * (size[axes[stage]] - 1))
    total = max(sum(n for _, n in parts) for parts in PARTS.values())
    out = pl.pallas_call(
        functools.partial(body, dims, Names()),
        out_shape=(
            jax.ShapeDtypeStruct((samples, rows, channels, cols), BF16),
            jax.ShapeDtypeStruct((total, LANES), BF16),
            jax.ShapeDtypeStruct((1, 2 * channels), F32),
            jax.ShapeDtypeStruct((1, 2 * channels), F32),
        ),
        in_specs=[anywhere] * 5 + [vmem] * 2,
        out_specs=(anywhere, anywhere, vmem, vmem),
        scratch_shapes=[
            pltpu.VMEM((rows + 2, channels, wide), BF16),
            pltpu.VMEM((rows + 2, channels, wide), BF16),
            pltpu.VMEM((rows, channels, wide), BF16),
            pltpu.VMEM((3, 3 * channels, 2 * channels), BF16),
            pltpu.VMEM((channels, channels), BF16),
            pltpu.VMEM((3, 2 * channels, 3 * channels), BF16),
            pltpu.VMEM((rows + 2, 2 * channels, wide), BF16),
            pltpu.VMEM((2 * channels, (rows + 2) * wide), BF16),
            pltpu.VMEM((3 * channels, rows * wide), BF16),
            pltpu.VMEM((4 * channels, wide), F32),
            pltpu.VMEM((2, rows, channels, wide), F32),
            pltpu.VMEM((rows, channels, wide), BF16),
            pltpu.VMEM((rows, channels, wide), BF16),
            pltpu.VMEM((12, channels, LANES), F32),
            pltpu.VMEM((8, channels, LANES), F32),
            pltpu.VMEM((2 * channels, LANES), F32),
            pltpu.VMEM((2 * channels, LANES), F32),
            pltpu.VMEM((64, 8, channels), F32),
            pltpu.VMEM((total, LANES), BF16),
            pltpu.VMEM((3, inbox[0], LANES), BF16),
            pltpu.VMEM((3, inbox[1], LANES), BF16),
            pltpu.VMEM((3, inbox[2], LANES), BF16),
            pltpu.VMEM((3 * stride[0], LANES), BF16),
            pltpu.VMEM((3 * stride[1], LANES), BF16),
            pltpu.VMEM((total, LANES), BF16),
            pltpu.SemaphoreType.DMA((150,)),
            pltpu.SemaphoreType.DMA((150,)),
            pltpu.SemaphoreType.DMA((16,)),
        ],
        compiler_params=pltpu.CompilerParams(
            collective_id=0, has_side_effects=True, vmem_limit_bytes=60 * 1024 * 1024
        ),
    )(
        turned(latents), turned(hint), turned(cotangent),
        conv_weight[0].transpose(0, 2, 1).reshape(3, 3 * channels, 2 * channels), ctrl_weight[0],
        norm_gain, norm_bias,
    )
    acts, conv, ctrl, gain, bias = pl.pallas_call(
        functools.partial(deliver, channels),
        out_shape=(
            jax.ShapeDtypeStruct((samples, rows, channels, cols), BF16),
            jax.ShapeDtypeStruct((9 * channels, 2 * channels), BF16),
            jax.ShapeDtypeStruct((channels, channels), F32),
            jax.ShapeDtypeStruct((1, 2 * channels), F32),
            jax.ShapeDtypeStruct((1, 2 * channels), F32),
        ),
        in_specs=[vmem] * 4,
        out_specs=(anywhere, anywhere, vmem, vmem, vmem),
        scratch_shapes=[
            pltpu.VMEM((3 * channels, LANES), BF16),
            pltpu.SemaphoreType.DMA((20,)),
        ],
        compiler_params=pltpu.CompilerParams(vmem_limit_bytes=24 * 1024 * 1024),
    )(*out)
    return (
        acts.reshape(1, samples, frames, rows, channels, cols).transpose(0, 1, 2, 3, 5, 4),
        conv.reshape(1, 9, channels, 2 * channels).transpose(0, 1, 3, 2),
        ctrl[None],
        gain,
        bias,
    )


def grid_of(mesh):
    space = mesh.shape["space"]
    columns = 4 if space >= 32 else 2
    return (space // columns, columns, mesh.shape["dp"])


def solution(mesh):
    return jax.shard_map(
        functools.partial(on_device, grid_of(mesh)),
        mesh=mesh,
        in_specs=(
            P("dp", None, "space", None, None),
            P("dp", None, "space", None, None),
            P("dp", None, "space", None, None),
            P("segment", None, None, None),
            P("segment", None, None),
            P("segment", None),
            P("segment", None),
        ),
        out_specs=(
            P("segment", "dp", None, "space", None, None),
            P("segment", None, None, None),
            P("segment", None, None),
            P("segment", None),
            P("segment", None),
        ),
        check_vma=False,
    )
```

time: 170 us -> 129 us (0.76)
  the two profiles are of different devices: /device:TPU:32 before, /device:TPU:1 now
where the time goes in v2:
time: 129 us
  Pallas kernels  124 us (96%)
  local copies, waits for them, and re-layouts  4.61 us (4%)
    pallas_call x1, Pallas kernels, on_device(): pl.pallas_call(functools.partial(body, dims, Names()), out_shape=(jax.Sha...  121 us
    unnamed x8, local copies, waits for them, and re-layouts  4.61 us
    pallas_call x1, Pallas kernels, on_device(): pl.pallas_call(functools.partial(deliver, channels), out_shape=(jax.Shape...  3 us

profile of v2, /device:TPU:1, one launch (start us, length us, event | category | flops | bytes accessed | tf_op | source)
XLA Modules:
  0.0 129.2 jit_solution(221210388241941348)
XLA Ops:
  0.6 120.7 %shard_map.110 = (bf16[2,4,320,128]{3,2,1,0:T(8,128)(2,1)}, bf16[16384,128]{1,0:T(8,128)(2,1)}, f32[1,640]{1,0:T(1,128)}, f32[1,640]{1,0:T(1,128)}) custom-call(bf16[2,4,320,128]{3,2,1,0:T(8,128)(2,1)} %bitcast.31, bf16[2,4,320,128]{3,2,1,0:T(8,128)(2,1)} %bitcast.32, bf16[2,4,320,128]{3,2,1,0:T(8,128)(2,1)} %bitcast.33, bf16[3,960,640]{2,1,0:T(8,128)(2,1)} %bitcast.30, ...), custom_call_target="tpu_custom_call" | custom-call | tf_op jit(solution)/shard_map/pallas_call | solution.py:692
  121.4 0.0 copy-start
  121.4 2.2 %copy-done = bf16[16384,128]{1,0:T(8,128)(2,1)S(1)} copy-done((bf16[16384,128]{1,0:T(8,128)(2,1)S(1)}, bf16[16384,128]{1,0:T(8,128)(2,1)}, u32[]{:S(2)}) %copy-start) | copy-done | bytes 4194328
  123.6 0.0 copy-start.1
  123.6 1.1 copy-done.1
  124.7 0.0 copy-start.2
  124.7 0.7 copy-done.2
  125.3 0.0 copy-start.3
  125.3 0.7 copy-done.3
  126.0 3.0 %shard_map.111 = (bf16[2,4,320,128]{3,2,1,0:T(8,128)(2,1)}, bf16[2880,640]{1,0:T(8,128)(2,1)}, f32[320,320]{1,0:T(8,128)}, f32[1,640]{1,0:T(1,128)}, f32[1,640]{1,0:T(1,128)}) custom-call(bf16[2,4,320,128]{3,2,1,0:T(8,128)(2,1)S(1)} %copy-done.1, bf16[16384,128]{1,0:T(8,128)(2,1)S(1)} %copy-done, f32[1,640]{1,0:T(1,128)S(1)} %copy-done.2, f32[1,640]{1,0:T(1,128)S(1)} %copy-done.3), custom_call_target="tpu_custom_call" | custom-call | tf_op jit(solution)/shard_map/pallas_call | solution.py:740
Async XLA Ops:
  121.4 2.2 %copy-start = (bf16[16384,128]{1,0:T(8,128)(2,1)S(1)}, bf16[16384,128]{1,0:T(8,128)(2,1)}, u32[]{:S(2)}) copy-start(bf16[16384,128]{1,0:T(8,128)(2,1)} %get-tuple-element.15.grads_in) | copy-start | bytes 12582916
  123.6 1.1 copy-start.1
  124.7 0.7 copy-start.2
  125.3 0.7 copy-start.3

commit v3 on v2

--- a/solution.py
+++ b/solution.py
@@ -459,9 +459,10 @@
             put(f"{name} {stage}", axes[stage], value)
             start(exchange(f"{name} {stage}", axes[stage]))
 
+        turn = (0, 1, 2) if halves == 1 else (1, 0, 2)
         small_start(0)
         for stage in range(3):
-            for p in range(3):
+            for p in turn:
                 wait(scatter_copies(p, halves, stage))
                 scatter_sum(p, halves, stage)
                 start(scatter_copies(p, halves, stage + 1) if stage < 2 else gather_copies(p, halves, 2))
@@ -471,7 +472,7 @@
                 if stage + 1 < len(axes):
                     small_start(stage + 1)
         for stage in (2, 1, 0):
-            for p in range(3):
+            for p in turn:
                 gather_wait(p, halves, stage)
                 if stage > 0:
                     start(gather_copies(p, halves, stage - 1))
@@ -637,38 +638,52 @@
 
 def deliver(
     channels, acts_in, grads_in, gain_in, bias_in,
-    acts_out, conv_out, ctrl_out, gain_out, bias_out, zeros_v, sem,
+    acts_out, conv_out, ctrl_out, gain_out, bias_out,
+    acts_v, grads_v, ctrl_v, gain_v, bias_v, zeros_v, load_sem, save_sem,
 ):
     seg = lax.axis_index("segment")
     high = 3 * channels
 
-    def copies(count):
-        out = [
-            pltpu.make_async_copy(acts_in, acts_out, sem.at[0]),
-        ]
+    def run(count):
+        base, last = 3 * count * high, channels - 2 * LANES
+        moves = [(grads_in.at[pl.ds(base, high), :], grads_v.at[pl.ds(base, high), :], None)]
+        for b in range(acts_v.shape[0]):
+            moves.append((acts_in.at[b], acts_v.at[b], acts_out.at[b]))
         for dr in range(3):
-            for j in range(5):
-                target = conv_out.at[pl.ds(dr * high, high), pl.ds(j * LANES, LANES)]
-                source = grads_in.at[pl.ds((dr * count + j) * high, high), :] if j < count else zeros_v
-                out.append(pltpu.make_async_copy(source, target, sem.at[1 + 5 * dr + j]))
-        return out
-
-    def run(count):
-        moves = copies(count)
-        for c in moves:
+            for k in range(count):
+                where = pl.ds((dr * count + k) * high, high)
+                target = conv_out.at[pl.ds(dr * high, high), pl.ds(k * LANES, LANES)]
+                moves.append((grads_in.at[where, :], grads_v.at[where, :], target))
+        moves.append((gain_in, gain_v, gain_out))
+        moves.append((bias_in, bias_v, bias_out))
+        loads = [pltpu.make_async_copy(src, mid, load_sem.at[n]) for n, (src, mid, _) in enumerate(moves)]
+        for c in loads:
             c.start()
-        gain_out[...] = gain_in[...]
-        bias_out[...] = bias_in[...]
-        base, last = 3 * count * high, channels - 2 * LANES
-        ctrl_out[:, 0:LANES] = grads_in[base:base + channels, :].astype(F32)
-        ctrl_out[:, LANES:2 * LANES] = grads_in[base + channels:base + 2 * channels, :].astype(F32)
-        ctrl_out[:, 2 * LANES:channels] = grads_in[base + 2 * channels:base + high, 0:last].astype(F32)
-        for c in moves:
+        saves = []
+        if count < 5:
+            zeros_v[...] = jnp.zeros(zeros_v.shape, BF16)
+            for dr in range(3):
+                for k in range(count, 5):
+                    target = conv_out.at[pl.ds(dr * high, high), pl.ds(k * LANES, LANES)]
+                    saves.append(pltpu.make_async_copy(zeros_v, target, save_sem.at[20 + 2 * dr + k - count]))
+            for c in saves:
+                c.start()
+        for n, (_, mid, target) in enumerate(moves):
+            loads[n].wait()
+            if target is None:
+                ctrl_v[:, 0:LANES] = grads_v[base:base + channels, :].astype(F32)
+                ctrl_v[:, LANES:2 * LANES] = grads_v[base + channels:base + 2 * channels, :].astype(F32)
+                ctrl_v[:, 2 * LANES:channels] = grads_v[base + 2 * channels:base + high, 0:last].astype(F32)
+                save = pltpu.make_async_copy(ctrl_v, ctrl_out, save_sem.at[n])
+            else:
+                save = pltpu.make_async_copy(mid, target, save_sem.at[n])
+            save.start()
+            saves.append(save)
+        for c in saves:
             c.wait()
 
     @pl.when(seg == 0)
     def _():
-        zeros_v[...] = jnp.zeros(zeros_v.shape, BF16)
         run(3)
 
     @pl.when(seg == 1)
@@ -746,13 +761,19 @@
             jax.ShapeDtypeStruct((1, 2 * channels), F32),
             jax.ShapeDtypeStruct((1, 2 * channels), F32),
         ),
-        in_specs=[vmem] * 4,
-        out_specs=(anywhere, anywhere, vmem, vmem, vmem),
+        in_specs=[anywhere] * 4,
+        out_specs=(anywhere,) * 5,
         scratch_shapes=[
+            pltpu.VMEM((samples, rows, channels, cols), BF16),
+            pltpu.VMEM((total, LANES), BF16),
+            pltpu.VMEM((channels, channels), F32),
+            pltpu.VMEM((1, 2 * channels), F32),
+            pltpu.VMEM((1, 2 * channels), F32),
             pltpu.VMEM((3 * channels, LANES), BF16),
             pltpu.SemaphoreType.DMA((20,)),
+            pltpu.SemaphoreType.DMA((26,)),
         ],
-        compiler_params=pltpu.CompilerParams(vmem_limit_bytes=24 * 1024 * 1024),
+        compiler_params=pltpu.CompilerParams(vmem_limit_bytes=60 * 1024 * 1024),
     )(*out)
     return (
         acts.reshape(1, samples, frames, rows, channels, cols).transpose(0, 1, 2, 3, 5, 4),

time: 129 us -> 123 us (0.953)
  local copies, waits for them, and re-layouts: 4.61 us -> 0 us
  Pallas kernels: 124 us -> 122 us
    unnamed x8 -> x0, local copies, waits for them, and re-layouts: 4.61 us -> none
    pallas_call x1, Pallas kernels: 121 us -> 118 us  [on_device(): pl.pallas_call(functools.partial(body, dims, Names()), out_shape=(jax.Sha...]
    pallas_call x1, Pallas kernels: 3 us -> 4.5 us  [on_device(): pl.pallas_call(functools.partial(deliver, channels), out_shape=(jax.Shape...]
where the time goes in v3:
time: 123 us
  Pallas kernels  122 us (99%)
    pallas_call x1, Pallas kernels, on_device(): pl.pallas_call(functools.partial(body, dims, Names()), out_shape=(jax.Sha...  118 us
    pallas_call x1, Pallas kernels, on_device(): pl.pallas_call(functools.partial(deliver, channels), out_shape=(jax.Shape...  4.5 us

profile of v3, /device:TPU:1, one launch (start us, length us, event | category | flops | bytes accessed | tf_op | source)
XLA Modules:
  0.0 123.0 jit_solution(8451450701270134396)
XLA Ops:
  0.6 117.7 %shard_map.110 = (bf16[2,4,320,128]{3,2,1,0:T(8,128)(2,1)}, bf16[16384,128]{1,0:T(8,128)(2,1)}, f32[1,640]{1,0:T(1,128)}, f32[1,640]{1,0:T(1,128)}) custom-call(bf16[2,4,320,128]{3,2,1,0:T(8,128)(2,1)} %bitcast.31, bf16[2,4,320,128]{3,2,1,0:T(8,128)(2,1)} %bitcast.32, bf16[2,4,320,128]{3,2,1,0:T(8,128)(2,1)} %bitcast.33, bf16[3,960,640]{2,1,0:T(8,128)(2,1)} %bitcast.30, ...), custom_call_target="tpu_custom_call" | custom-call | tf_op jit(solution)/shard_map/pallas_call | solution.py:707
  118.3 4.5 %shard_map.111 = (bf16[2,4,320,128]{3,2,1,0:T(8,128)(2,1)}, bf16[2880,640]{1,0:T(8,128)(2,1)}, f32[320,320]{1,0:T(8,128)}, f32[1,640]{1,0:T(1,128)}, f32[1,640]{1,0:T(1,128)}) custom-call(bf16[2,4,320,128]{3,2,1,0:T(8,128)(2,1)} %get-tuple-element.14.acts_in, bf16[16384,128]{1,0:T(8,128)(2,1)} %get-tuple-element.15.grads_in, ...), custom_call_target="tpu_custom_call" | custom-call | tf_op jit(solution)/shard_map/pallas_call | solution.py:755
